TPU v7x, 512 devices: a whole 4x4x16 slice. The times are simulated.
512 devices in a mesh: ctx: 128 (over x_lo, z, y), head: 4 (over x_hi, core).
Axes of the slice: x: 4 (x_hi: 2, x_lo: 2; x = x_hi * 2 + x_lo), y: 4, z: 16, core: 2. Of those that a mesh axis runs over, the one named last changes fastest.
Arguments:
- queries: bfloat16 [49152, 2048], P('ctx', 'head'), may hold values from -10 to 10, as said below
- key_rows: bfloat16 [49152, 2048], P('ctx', 'head'), may hold values from -10 to 10, as said below
- value_rows: bfloat16 [49152, 2048], P('ctx', 'head'), may hold values from -6 to 6
- out_weight: bfloat16 [2048, 2048], P('head'), may hold values from -0.125 to 0.125
- cotangent: bfloat16 [49152, 2048], P('ctx', 'head'), may hold values from -6 to 6
- offsets: int32 [2056], replicated, may hold values from 0 to 394560, as said below
Outputs:
- mixed: bfloat16 [49152, 2048], P('ctx', 'head')
- grad_queries: bfloat16 [49152, 2048], P('ctx', 'head')
- grad_keys: bfloat16 [49152, 2048], P('ctx', 'head')
- grad_values: bfloat16 [49152, 2048], P('ctx', 'head')
Inputs may be any that keep to these rules, and one draw needn't show every extreme that they name: offsets start at 0 and increase; consecutive entries differ by 1 to 192 except before the last entry, which is (2055) * 192 and lies beyond the history, as does the entry before it. `queries`: real values. `key_rows`: real values.
All inputs are finite; a program needn't handle non-finite values.
Results may differ from a plain program's by a relative error of at most 0.018.
Values may be sent and summed in bfloat16 or wider, within the bound.
A program may use at most 64 MiB of HBM per device.

v0:
```python
from functools import reduce
import math

import jax
import jax.numpy as jnp
from jax import lax
from jax.sharding import PartitionSpec as P

HD = 128
REACH = 2
PREV = 3


NEG_FILL = -1e30


def passed_along(shard, axis, by):
    length = lax.axis_size(axis)
    pairs = [(i, i + by) for i in range(length) if 0 <= i + by < length]
    return lax.ppermute(shard, axis, pairs)


def episode_ids(positions, offsets):
    hit_count = jnp.sum((offsets[None, :] <= positions[:, None]).astype(jnp.int32), axis=1)
    return hit_count - 1


def window_mask(query_pos, query_ep, key_pos, offsets):
    key_ep = episode_ids(key_pos, offsets)
    return (
        (key_pos[None, :] <= query_pos[:, None])
        & (key_pos[None, :] >= 0)
        & (query_ep[:, None] - key_ep[None, :] <= PREV)
    )


def score_tile(query_tile, key_tile, tile_mask, score_scale):
    raw = (
        jnp.einsum("qhd,khd->hqk", query_tile, key_tile, preferred_element_type=jnp.float32)
        * score_scale
    )
    return jnp.where(tile_mask[None], raw, NEG_FILL)


def mix_values(weights, value_tile):
    return jnp.einsum(
        "hqk,khd->qhd", weights.astype(jnp.bfloat16), value_tile, preferred_element_type=jnp.float32
    )


def scores_grad(weights, grad_tile, value_tile, row_delta, score_scale):
    grad_probs = jnp.einsum(
        "qhd,khd->hqk", grad_tile, value_tile, preferred_element_type=jnp.float32
    )
    return (score_scale * weights * (grad_probs - row_delta[:, :, None])).astype(jnp.bfloat16)


def tile_backward(weights, query_tile, key_tile, value_tile, grad_tile, row_delta, score_scale):
    grad_scores = scores_grad(weights, grad_tile, value_tile, row_delta, score_scale)
    part_q = jnp.einsum("hqk,khd->qhd", grad_scores, key_tile, preferred_element_type=jnp.float32)
    part_k = jnp.einsum("hqk,qhd->khd", grad_scores, query_tile, preferred_element_type=jnp.float32)
    part_v = jnp.einsum(
        "hqk,qhd->khd", weights.astype(jnp.bfloat16), grad_tile, preferred_element_type=jnp.float32
    )
    return (part_q, part_k, part_v)


def per_device(queries, key_rows, value_rows, out_weight, cotangent, offsets):
    row_count = queries.shape[0]
    head_cols = queries.shape[1]
    head_count = head_cols // HD
    score_scale = 1.0 / math.sqrt(HD)
    my_index = lax.axis_index("ctx")
    own_pos = my_index * row_count + jnp.arange(row_count, dtype=jnp.int32)
    own_ep = episode_ids(own_pos, offsets)
    query_heads = queries.reshape(row_count, head_count, HD)
    own_keys = key_rows.reshape(row_count, head_count, HD)
    own_values = value_rows.reshape(row_count, head_count, HD)
    key_tiles = []
    value_tiles = []
    tile_masks = []
    for distance in range(REACH, 0, -1):
        came_keys, came_values = passed_along((key_rows, value_rows), "ctx", distance)
        key_tiles.append(came_keys.reshape(row_count, head_count, HD))
        value_tiles.append(came_values.reshape(row_count, head_count, HD))
        tile_masks.append(window_mask(own_pos, own_ep, own_pos - distance * row_count, offsets))
    key_tiles.append(own_keys)
    value_tiles.append(own_values)
    tile_masks.append(window_mask(own_pos, own_ep, own_pos, offsets))
    blank_rows = jnp.zeros((row_count, head_count, HD), jnp.float32)
    scores = []
    for tile_index in range(REACH + 1):
        scores.append(
            score_tile(query_heads, key_tiles[tile_index], tile_masks[tile_index], score_scale)
        )
    row_max = reduce(jnp.maximum, [jnp.max(tile_scores, axis=2) for tile_scores in scores])
    row_total = reduce(
        jnp.add,
        [jnp.sum(jnp.exp(tile_scores - row_max[:, :, None]), axis=2) for tile_scores in scores],
    )
    log_total = row_max + jnp.log(row_total)
    attn_probs = [
        jnp.where(
            tile_masks[tile_index][None], jnp.exp(scores[tile_index] - log_total[:, :, None]), 0.0
        )
        for tile_index in range(REACH + 1)
    ]
    attended = blank_rows
    for tile_index in range(REACH + 1):
        attended = attended + mix_values(attn_probs[tile_index], value_tiles[tile_index])
    attended_b = attended.reshape(row_count, head_cols).astype(jnp.bfloat16)
    projected = jnp.dot(attended_b, out_weight, preferred_element_type=jnp.float32)
    mixed = lax.psum_scatter(projected, "head", scatter_dimension=1, tiled=True).astype(
        jnp.bfloat16
    )
    grad_out = lax.dot_general(
        lax.all_gather(cotangent, "head", axis=1, tiled=True),
        out_weight,
        (((1,), (1,)), ((), ())),
        preferred_element_type=jnp.float32,
    ).astype(jnp.bfloat16)
    grad_heads = grad_out.reshape(row_count, head_count, HD)
    row_delta = jnp.einsum(
        "qhd,qhd->hq",
        grad_heads,
        attended_b.reshape(row_count, head_count, HD),
        preferred_element_type=jnp.float32,
    )
    grad_q = blank_rows
    sent_keys = []
    sent_values = []
    for tile_index in range(REACH + 1):
        part_q, part_k, part_v = tile_backward(
            attn_probs[tile_index],
            query_heads,
            key_tiles[tile_index],
            value_tiles[tile_index],
            grad_heads,
            row_delta,
            score_scale,
        )
        grad_q = grad_q + part_q
        sent_keys.append(part_k)
        sent_values.append(part_v)
    grad_k = sent_keys[REACH]
    grad_v = sent_values[REACH]
    for distance in range(1, REACH + 1):
        came_k, came_v = passed_along(
            (sent_keys[REACH - distance], sent_values[REACH - distance]), "ctx", -distance
        )
        grad_k = grad_k + came_k
        grad_v = grad_v + came_v
    grad_queries = grad_q.reshape(row_count, head_cols).astype(jnp.bfloat16)
    grad_keys = grad_k.reshape(row_count, head_cols).astype(jnp.bfloat16)
    grad_values = grad_v.reshape(row_count, head_cols).astype(jnp.bfloat16)
    return (mixed, grad_queries, grad_keys, grad_values)


def solution(mesh):
    in_specs = (
        P("ctx", "head"),
        P("ctx", "head"),
        P("ctx", "head"),
        P("head", None),
        P("ctx", "head"),
        P(),
    )
    out_specs = (P("ctx", "head"), P("ctx", "head"), P("ctx", "head"), P("ctx", "head"))
    return jax.shard_map(
        per_device, mesh=mesh, in_specs=in_specs, out_specs=out_specs, check_vma=False
    )
```

profile of v0, /device:TPU:483, one launch (start us, length us, event | category | flops | bytes accessed | tf_op | source)
XLA Modules:
  0.0 195.7 jit_solution(10340296261463767993)
XLA Ops:
  8.6 4.8 %collective-permute-start = (bf16[384,512]{0,1:T(8,128)(2,1)S(1)}, bf16[384,512]{0,1:T(8,128)(2,1)}, u32[]{:S(2)}, u32[]{:S(2)}) collective-permute-start(bf16[384,512]{0,1:T(8,128)(2,1)S(1)} %copy.92), channel_id=1, source_target_pairs={{0,8},{4,12},{8,16},{12,20},{16,24},{20,28},{24,32},{28,36},{32,40... | collective-permute-start | bytes 1179656 | tf_op jit(solution)/shard_map/ppermute | solution.py:20
  13.4 2.3 %collective-permute-start.1 = (bf16[384,512]{0,1:T(8,128)(2,1)S(1)}, bf16[384,512]{0,1:T(8,128)(2,1)}, u32[]{:S(2)}, u32[]{:S(2)}) collective-permute-start(bf16[384,512]{0,1:T(8,128)(2,1)S(1)} %copy.92), channel_id=1, source_target_pairs={{0,4},{4,8},{8,12},{12,16},{16,20},{20,24},{24,28},{28,32},{32,36}... | collective-permute-start | bytes 1179656 | tf_op jit(solution)/shard_map/ppermute | solution.py:20
  15.7 1.9 collective-permute-start.3
  17.7 1.9 collective-permute-start.2
  19.7 1.9 convert_reduce_fusion
  22.5 3.2 %fusion.49 = (f32[4,384]{1,0:T(4,128)S(1)}, f32[4,384,384]{1,2,0:T(8,128)}) fusion(bf16[384,4,128]{0,2,1:T(8,128)(2,1)S(1)} %bitcast.117, pred[384,384]{0,1:T(8,128)(4,1)S(1)} %get-tuple-element.23, bf16[384,512]{1,0:T(8,128)(2,1)} %param.6), kind=kOutput, calls=%fused_computation.80 | convolution fusion | flops 152762880 | bytes 3299328 | tf_op jit(solution)/shard_map/qhd,khd->hqk/dot_general | solution.py:39
  25.7 23.0 %collective-permute-done.3 = bf16[384,512]{1,0:T(8,128)(2,1)} collective-permute-done((bf16[384,512]{1,0:T(8,128)(2,1)}, bf16[384,512]{1,0:T(8,128)(2,1)}, u32[]{:S(2)}, u32[]{:S(2)}) %collective-permute-start.3) | collective-permute-done | bytes 393248 | tf_op jit(solution)/shard_map/ppermute | solution.py:20
  48.7 1.9 copy.102
  50.6 1.9 copy.100
  52.6 1.6 fusion.50
  54.2 2.1 %fusion.51 = (f32[4,384]{1,0:T(4,128)S(1)}, f32[4,384,384]{1,2,0:T(8,128)S(1)}) fusion(bf16[384,4,128]{0,2,1:T(8,128)(2,1)} %bitcast.3, pred[384,384]{0,1:T(8,128)(4,1)S(1)} %get-tuple-element.22, bf16[384,512]{1,0:T(8,128)(2,1)S(1)} %copy-done.7), kind=kOutput, calls=%fused_computation.82 | convolution fusion | flops 152762880 | bytes 3299328 | tf_op jit(solution)/shard_map/qhd,khd->hqk/dot_general | solution.py:39
  58.2 1.5 fusion.16
  61.1 3.2 %convolution_convert_fusion = bf16[384,512]{1,0:T(8,128)(2,1)} fusion(bf16[384,2048]{1,0:T(8,128)(2,1)} %all-gather.2.cloned.1.call-done, bf16[512,2048]{1,0:T(8,128)(2,1)S(1)} %copy-done), kind=kOutput, calls=%fused_computation.36 | convolution fusion | flops 805502976 | bytes 4063232 | tf_op jit(solution)/shard_map/dot_general | solution.py:116
  66.4 2.3 %copy.146 = f32[4,384,128]{1,2,0:T(8,128)} copy(f32[4,384,128]{2,0,1:T(4,128)} %bitcast_convert_fusion) | data formatting | bytes 1572864
  68.7 3.1 %multiply_reduce_fusion = (f32[4,384]{1,0:T(4,128)S(1)}, bf16[4,384,128]{1,2,0:T(8,128)(2,1)S(1)}) fusion(f32[4,384,128]{1,2,0:T(8,128)} %copy.146, f32[4,384,128]{1,2,0:T(8,128)} %fusion.16, f32[4,384,128]{1,2,0:T(8,128)} %fusion.36, bf16[384,4,128]{0,2,1:T(8,128)(2,1)} %bitcast.119, f32[4,384,384]{1,2,0:T(8,128)} %copy-done.5, ...), kind=kOutput, calls=%fused_computation.37 | convolution fusion | flops 153942528 | bytes 5664768 | tf_op jit(solution)/shard_map/hqk,khd->qhd/dot_general | solution.py:46
  71.7 2.6 %fusion.52 = f32[384,2048]{1,0:T(8,128)} fusion(bf16[384,512]{0,1:T(8,128)(2,1)S(1)} %bitcast.126, bf16[512,2048]{1,0:T(8,128)(2,1)S(1)} %copy-done), kind=kOutput, calls=%fused_computation.83 | convolution fusion | flops 805306368 | bytes 5636096 | tf_op jit(solution)/shard_map/dot_general | solution.py:112
  74.7 3.3 %convolution_bitcast_fusion.1 = f32[384,4,128]{0,2,1:T(8,128)} fusion(bf16[384,4,128]{0,2,1:T(8,128)(2,1)S(1)} %copy.125, f32[4,384,384]{1,2,0:T(8,128)} %copy-done.3, f32[4,384]{1,0:T(4,128)S(1)} %log_add_fusion, pred[384,384]{0,1:T(8,128)(4,1)} %copy-done.11), kind=kOutput, calls=%fused_computation.19 | convolution fusion | flops 152764416 | bytes 3692544 | tf_op jit(solution)/shard_map/hqk,qhd->khd/dot_general | solution.py:62
  78.0 7.8 %collective-permute-start.6 = (f32[384,4,128]{0,2,1:T(8,128)}, f32[384,4,128]{0,2,1:T(8,128)}, u32[]{:S(2)}, u32[]{:S(2)}) collective-permute-start(f32[384,4,128]{0,2,1:T(8,128)} %convolution_bitcast_fusion.1), channel_id=1, source_target_pairs={{4,0},{8,4},{12,8},{16,12},{20,16},{24,20},{28,24},{32,28},{36,32}... | collective-permute-start | bytes 2359304 | tf_op jit(solution)/shard_map/ppermute | solution.py:20
  85.8 1.5 convolution_bitcast_fusion
  87.3 5.4 %collective-permute-start.7 = (f32[384,4,128]{0,2,1:T(8,128)}, f32[384,4,128]{0,2,1:T(8,128)}, u32[]{:S(2)}, u32[]{:S(2)}) collective-permute-start(f32[384,4,128]{0,2,1:T(8,128)} %convolution_bitcast_fusion), channel_id=1, source_target_pairs={{8,0},{12,4},{16,8},{20,12},{24,16},{28,20},{32,24},{36,28},{40,32... | collective-permute-start | bytes 2359304 | tf_op jit(solution)/shard_map/ppermute | solution.py:20
  93.8 1.5 convolution_bitcast_fusion.3
  95.3 2.1 %collective-permute-start.5 = (f32[384,4,128]{0,2,1:T(8,128)}, f32[384,4,128]{0,2,1:T(8,128)}, u32[]{:S(2)}, u32[]{:S(2)}) collective-permute-start(f32[384,4,128]{0,2,1:T(8,128)} %convolution_bitcast_fusion.3), channel_id=1, source_target_pairs={{8,0},{12,4},{16,8},{20,12},{24,16},{28,20},{32,24},{36,28},{40,32... | collective-permute-start | bytes 2359304 | tf_op jit(solution)/shard_map/ppermute | solution.py:20
  99.8 2.5 %collective-permute-start.4 = (f32[384,4,128]{0,2,1:T(8,128)}, f32[384,4,128]{0,2,1:T(8,128)}, u32[]{:S(2)}, u32[]{:S(2)}) collective-permute-start(f32[384,4,128]{0,2,1:T(8,128)} %convolution_bitcast_fusion.4), channel_id=1, source_target_pairs={{4,0},{8,4},{12,8},{16,12},{20,16},{24,20},{28,24},{32,28},{36,32}... | collective-permute-start | bytes 2359304 | tf_op jit(solution)/shard_map/ppermute | solution.py:20
  103.3 1.8 fusion.53
  107.9 4.7 %collective-permute-done.6 = f32[384,4,128]{0,2,1:T(8,128)} collective-permute-done((f32[384,4,128]{0,2,1:T(8,128)}, f32[384,4,128]{0,2,1:T(8,128)}, u32[]{:S(2)}, u32[]{:S(2)}) %collective-permute-start.6) | collective-permute-done | bytes 786464 | tf_op jit(solution)/shard_map/ppermute | solution.py:20
  112.5 17.4 %collective-permute-done.7 = f32[384,4,128]{0,2,1:T(8,128)} collective-permute-done((f32[384,4,128]{0,2,1:T(8,128)}, f32[384,4,128]{0,2,1:T(8,128)}, u32[]{:S(2)}, u32[]{:S(2)}) %collective-permute-start.7) | collective-permute-done | bytes 786464 | tf_op jit(solution)/shard_map/ppermute | solution.py:20
  129.9 2.7 %fusion.11 = bf16[384,4,128]{0,2,1:T(8,128)(2,1)S(1)} fusion(f32[384,4,128]{0,2,1:T(8,128)} %collective-permute-done.7, f32[384,4,128]{0,2,1:T(8,128)} %collective-permute-done.6, bf16[384,4,128]{0,2,1:T(8,128)(2,1)S(1)} %copy.125, f32[4,384,384]{1,2,0:T(8,128)} %get-tuple-element.26, f32[4,384]{1,0:T(4,128)S(1)} %log_add_fusion, ...), kind=kOutput, calls=%fused_computation.34 | convolution fusion | flops 153354240 | bytes 4872192 | tf_op jit(solution)/shard_map/hqk,qhd->khd/dot_general | solution.py:62
  133.5 13.3 %collective-permute-done.5 = f32[384,4,128]{0,2,1:T(8,128)} collective-permute-done((f32[384,4,128]{0,2,1:T(8,128)}, f32[384,4,128]{0,2,1:T(8,128)}, u32[]{:S(2)}, u32[]{:S(2)}) %collective-permute-start.5) | collective-permute-done | bytes 786464 | tf_op jit(solution)/shard_map/ppermute | solution.py:20
  146.7 16.9 %collective-permute-done.4 = f32[384,4,128]{0,2,1:T(8,128)} collective-permute-done((f32[384,4,128]{0,2,1:T(8,128)}, f32[384,4,128]{0,2,1:T(8,128)}, u32[]{:S(2)}, u32[]{:S(2)}) %collective-permute-start.4) | collective-permute-done | bytes 786464 | tf_op jit(solution)/shard_map/ppermute | solution.py:20
  163.6 2.3 %fusion.12 = bf16[384,4,128]{0,2,1:T(8,128)(2,1)S(1)} fusion(f32[384,4,128]{0,2,1:T(8,128)} %collective-permute-done.5, f32[384,4,128]{0,2,1:T(8,128)} %collective-permute-done.4, bf16[4,384,384]{1,2,0:T(8,128)(2,1)} %copy-done.8, bf16[384,512]{1,0:T(8,128)(2,1)S(1)} %copy-done.7), kind=kOutput, calls=%fused_computation.35 | convolution fusion | flops 151584768 | bytes 3538944 | tf_op jit(solution)/shard_map/hqk,qhd->khd/dot_general | solution.py:61
  166.8 20.1 %reduce-scatter.2.cloned.1.call-done = f32[384,512]{1,0:T(8,128)} async-done(((f32[384,2048]{1,0:T(8,128)}), f32[384,512]{1,0:T(8,128)}) %reduce-scatter.2.cloned.1.call-update) | async-done | bytes 786448 | tf_op jit(solution)/shard_map/reduce_scatter | solution.py:113
  186.9 1.9 convert_element_type.78
  (75 shorter events, 16.9 us)
Async XLA Ops:
  7.2 53.9 %copy-start = (bf16[512,2048]{1,0:T(8,128)(2,1)S(1)}, bf16[512,2048]{1,0:T(8,128)(2,1)}, u32[]{:S(2)}) copy-start(bf16[512,2048]{1,0:T(8,128)(2,1)} %param.9) | copy-start | bytes 6291460
  7.2 53.9 %all-gather.2.cloned.1.call-start = ((), (), s32[]{:S(2)}) async-start(), calls=%async_computation.2 | async-start | bytes 1966080 | tf_op jit(solution)/shard_map/all_gather | solution.py:117
  8.6 42.1 %copy-start.9 = (bf16[384,512]{0,1:T(8,128)(2,1)}, bf16[384,512]{0,1:T(8,128)(2,1)S(1)}, u32[]{:S(2)}) copy-start(bf16[384,512]{0,1:T(8,128)(2,1)S(1)} %copy.92) | copy-start | bytes 1179652
  8.6 44.0 %collective-permute-start = (bf16[384,512]{0,1:T(8,128)(2,1)S(1)}, bf16[384,512]{0,1:T(8,128)(2,1)}, u32[]{:S(2)}, u32[]{:S(2)}) collective-permute-start(bf16[384,512]{0,1:T(8,128)(2,1)S(1)} %copy.92), channel_id=1, source_target_pairs={{0,8},{4,12},{8,16},{12,20},{16,24},{20,28},{24,32},{28,36},{32,40... | collective-permute-start | bytes 1179656 | tf_op jit(solution)/shard_map/ppermute | solution.py:20
  13.4 40.8 %collective-permute-start.1 = (bf16[384,512]{0,1:T(8,128)(2,1)S(1)}, bf16[384,512]{0,1:T(8,128)(2,1)}, u32[]{:S(2)}, u32[]{:S(2)}) collective-permute-start(bf16[384,512]{0,1:T(8,128)(2,1)S(1)} %copy.92), channel_id=1, source_target_pairs={{0,4},{4,8},{8,12},{12,16},{16,20},{20,24},{24,28},{28,32},{32,36}... | collective-permute-start | bytes 1179656 | tf_op jit(solution)/shard_map/ppermute | solution.py:20
  15.7 33.0 %collective-permute-start.3 = (bf16[384,512]{1,0:T(8,128)(2,1)}, bf16[384,512]{1,0:T(8,128)(2,1)}, u32[]{:S(2)}, u32[]{:S(2)}) collective-permute-start(bf16[384,512]{1,0:T(8,128)(2,1)} %param.8), channel_id=1, source_target_pairs={{0,4},{4,8},{8,12},{12,16},{16,20},{20,24},{24,28},{28,32},{32,36}... | collective-permute-start | bytes 1179656 | tf_op jit(solution)/shard_map/ppermute | solution.py:20
  17.7 33.0 %collective-permute-start.2 = (bf16[384,512]{1,0:T(8,128)(2,1)}, bf16[384,512]{1,0:T(8,128)(2,1)}, u32[]{:S(2)}, u32[]{:S(2)}) collective-permute-start(bf16[384,512]{1,0:T(8,128)(2,1)} %param.8), channel_id=1, source_target_pairs={{0,8},{4,12},{8,16},{12,20},{16,24},{20,28},{24,32},{28,36},{32,40... | collective-permute-start | bytes 1179656 | tf_op jit(solution)/shard_map/ppermute | solution.py:20
  19.6 167.3 %reduce-scatter.2.cloned.1.call-start = ((), (), s32[]{:S(2)}) async-start(), calls=%async_computation.1 | async-start | bytes 3932160 | tf_op jit(solution)/shard_map/reduce_scatter | solution.py:113
  22.5 30.1 %copy-start.13 = (pred[384,384]{0,1:T(8,128)(4,1)}, pred[384,384]{0,1:T(8,128)(4,1)S(1)}, u32[]{:S(2)}) copy-start(pred[384,384]{0,1:T(8,128)(4,1)S(1)} %get-tuple-element.24) | copy-start | bytes 442372
  22.5 37.1 %copy-start.11 = (pred[384,384]{0,1:T(8,128)(4,1)}, pred[384,384]{0,1:T(8,128)(4,1)S(1)}, u32[]{:S(2)}) copy-start(pred[384,384]{0,1:T(8,128)(4,1)S(1)} %get-tuple-element.22) | copy-start | bytes 442372
  22.5 30.1 %copy-start.7 = (bf16[384,512]{1,0:T(8,128)(2,1)S(1)}, bf16[384,512]{1,0:T(8,128)(2,1)}, u32[]{:S(2)}) copy-start(bf16[384,512]{1,0:T(8,128)(2,1)} %param.6) | copy-start | bytes 1179652
  54.2 3.6 %copy-start.5 = (f32[4,384,384]{1,2,0:T(8,128)}, f32[4,384,384]{1,2,0:T(8,128)S(1)}, u32[]{:S(2)}) copy-start(f32[4,384,384]{1,2,0:T(8,128)S(1)} %get-tuple-element.28) | copy-start | bytes 7077892
  54.2 2.6 %copy-start.1 = (f32[4,384,384]{1,2,0:T(8,128)S(1)}, f32[4,384,384]{1,2,0:T(8,128)}, u32[]{:S(2)}) copy-start(f32[4,384,384]{1,2,0:T(8,128)} %get-tuple-element.26) | copy-start | bytes 7077892
  56.3 3.3 %copy-start.3 = (f32[4,384,384]{1,2,0:T(8,128)}, f32[4,384,384]{1,2,0:T(8,128)S(1)}, u32[]{:S(2)}) copy-start(f32[4,384,384]{1,2,0:T(8,128)S(1)} %get-tuple-element.30) | copy-start | bytes 7077892
  56.9 1.3 copy-start.19
  57.8 1.8 copy-start.17
  64.2 4.4 %copy-start.14 = (pred[384,384]{0,1:T(8,128)(4,1)S(1)}, pred[384,384]{0,1:T(8,128)(4,1)}, u32[]{:S(2)}) copy-start(pred[384,384]{0,1:T(8,128)(4,1)} %copy-done.13) | copy-start | bytes 442372
  74.7 11.1 %copy-start.6 = (f32[4,384,384]{1,2,0:T(8,128)S(1)}, f32[4,384,384]{1,2,0:T(8,128)}, u32[]{:S(2)}) copy-start(f32[4,384,384]{1,2,0:T(8,128)} %copy-done.5) | copy-start | bytes 7077892
  74.7 11.1 %copy-start.15 = (pred[384,384]{0,1:T(8,128)(4,1)S(1)}, pred[384,384]{0,1:T(8,128)(4,1)}, u32[]{:S(2)}) copy-start(pred[384,384]{0,1:T(8,128)(4,1)} %copy-done.13) | copy-start | bytes 442372
  78.0 14.8 %copy-start.16 = (bf16[384,512]{0,1:T(8,128)(2,1)S(1)}, bf16[384,512]{0,1:T(8,128)(2,1)}, u32[]{:S(2)}) copy-start(bf16[384,512]{0,1:T(8,128)(2,1)} %copy.100) | copy-start | bytes 1179652
  78.0 34.5 %collective-permute-start.6 = (f32[384,4,128]{0,2,1:T(8,128)}, f32[384,4,128]{0,2,1:T(8,128)}, u32[]{:S(2)}, u32[]{:S(2)}) collective-permute-start(f32[384,4,128]{0,2,1:T(8,128)} %convolution_bitcast_fusion.1), channel_id=1, source_target_pairs={{4,0},{8,4},{12,8},{16,12},{20,16},{24,20},{28,24},{32,28},{36,32}... | collective-permute-start | bytes 2359304 | tf_op jit(solution)/shard_map/ppermute | solution.py:20
  87.3 42.6 %collective-permute-start.7 = (f32[384,4,128]{0,2,1:T(8,128)}, f32[384,4,128]{0,2,1:T(8,128)}, u32[]{:S(2)}, u32[]{:S(2)}) collective-permute-start(f32[384,4,128]{0,2,1:T(8,128)} %convolution_bitcast_fusion), channel_id=1, source_target_pairs={{8,0},{12,4},{16,8},{20,12},{24,16},{28,20},{32,24},{36,28},{40,32... | collective-permute-start | bytes 2359304 | tf_op jit(solution)/shard_map/ppermute | solution.py:20
  92.8 4.6 %copy-start.12 = (pred[384,384]{0,1:T(8,128)(4,1)S(1)}, pred[384,384]{0,1:T(8,128)(4,1)}, u32[]{:S(2)}) copy-start(pred[384,384]{0,1:T(8,128)(4,1)} %copy-done.11) | copy-start | bytes 442372
  92.8 4.6 %copy-start.18 = (bf16[384,512]{0,1:T(8,128)(2,1)S(1)}, bf16[384,512]{0,1:T(8,128)(2,1)}, u32[]{:S(2)}) copy-start(bf16[384,512]{0,1:T(8,128)(2,1)} %copy.102) | copy-start | bytes 1179652
  93.8 3.7 %copy-start.4 = (f32[4,384,384]{1,2,0:T(8,128)S(1)}, f32[4,384,384]{1,2,0:T(8,128)}, u32[]{:S(2)}) copy-start(f32[4,384,384]{1,2,0:T(8,128)} %copy-done.3) | copy-start | bytes 7077892
  95.3 51.4 %collective-permute-start.5 = (f32[384,4,128]{0,2,1:T(8,128)}, f32[384,4,128]{0,2,1:T(8,128)}, u32[]{:S(2)}, u32[]{:S(2)}) collective-permute-start(f32[384,4,128]{0,2,1:T(8,128)} %convolution_bitcast_fusion.3), channel_id=1, source_target_pairs={{8,0},{12,4},{16,8},{20,12},{24,16},{28,20},{32,24},{36,28},{40,32... | collective-permute-start | bytes 2359304 | tf_op jit(solution)/shard_map/ppermute | solution.py:20
  97.4 4.9 %copy-start.20 = (bf16[384,512]{1,0:T(8,128)(2,1)S(1)}, bf16[384,512]{1,0:T(8,128)(2,1)}, u32[]{:S(2)}) copy-start(bf16[384,512]{1,0:T(8,128)(2,1)} %param.8) | copy-start | bytes 1179652
  98.4 4.0 %copy-start.2 = (f32[4,384,384]{1,2,0:T(8,128)S(1)}, f32[4,384,384]{1,2,0:T(8,128)}, u32[]{:S(2)}) copy-start(f32[4,384,384]{1,2,0:T(8,128)} %get-tuple-element.26) | copy-start | bytes 7077892
  99.8 63.8 %collective-permute-start.4 = (f32[384,4,128]{0,2,1:T(8,128)}, f32[384,4,128]{0,2,1:T(8,128)}, u32[]{:S(2)}, u32[]{:S(2)}) collective-permute-start(f32[384,4,128]{0,2,1:T(8,128)} %convolution_bitcast_fusion.4), channel_id=1, source_target_pairs={{4,0},{8,4},{12,8},{16,12},{20,16},{24,20},{28,24},{32,28},{36,32}... | collective-permute-start | bytes 2359304 | tf_op jit(solution)/shard_map/ppermute | solution.py:20
  103.3 2.2 %copy-start.8 = (bf16[4,384,384]{1,2,0:T(8,128)(2,1)}, bf16[4,384,384]{1,2,0:T(8,128)(2,1)S(1)}, u32[]{:S(2)}) copy-start(bf16[4,384,384]{1,2,0:T(8,128)(2,1)S(1)} %multiply_convert_fusion) | copy-start | bytes 3538948
  103.3 1.8 copy-start.10
Sparse Core Ops, SparseCore 0:
  19.7 32.5 all-gather.1
  74.5 112.3 reduce-scatter.1
where the time goes:
time: 197 us; the launch traced here: 196 us
  waiting for transfers between devices  95.2 us (48%)
  matrix products  37.8 us (19%)
  starting transfers between devices  28.9 us (15%)
  between operations  14.5 us (7%)
  local copies, waits for them, and re-layouts  12.6 us (6%)
  other arithmetic  6.62 us (3%)
    ppermute x8, waiting for transfers between devices, passed_along(): return lax.ppermute(shard, axis, pairs)  75.1 us
    ppermute x8, starting transfers between devices, passed_along(): return lax.ppermute(shard, axis, pairs)  28.8 us
    reduce_scatter x1, waiting for transfers between devices, per_device(): lax.psum_scatter(projected, 'head', scatter_dimension=1, tiled=True)  20.1 us
    dot_general x3, matrix products, tile_backward(): jnp.einsum('hqk,qhd->khd', weights.astype(jnp.bfloat16), grad_tile, prefe...  7.47 us
    unnamed x47, local copies, waits for them, and re-layouts  7.35 us
    dot_general x3, matrix products, score_tile(): jnp.einsum('qhd,khd->hqk', query_tile, key_tile, preferred_element_type=j...  6.93 us
    dot_general x3, matrix products, mix_values(): jnp.einsum('hqk,khd->qhd', weights.astype(jnp.bfloat16), value_tile, pref...  5.96 us
    dot_general x3, matrix products, tile_backward(): jnp.einsum('hqk,qhd->khd', grad_scores, query_tile, preferred_element_typ...  5.27 us
  transfers between devices with their start and end apart: 10, of which 6 were waited for; matrix products, arithmetic and copies ran while one was open for 20% of the time, Pallas kernels for 0%

commit v1 on v0

v1 whole, which is shorter than its diff:
```python
import functools
import math

import jax
import jax.numpy as jnp
from jax import lax
from jax.experimental import pallas as pl
from jax.experimental.pallas import tpu as pltpu
from jax.sharding import PartitionSpec as P

HD = 128
PREV = 3
NEG_FILL = -1e30
LOG2E = math.log2(math.e)
F32 = jnp.float32
BF16 = jnp.bfloat16
MESH = pl.DeviceIdType.MESH


def dot_nn(a, b):
    return lax.dot_general(a, b, (((1,), (0,)), ((), ())), preferred_element_type=F32)


def dot_nt(a, b):
    return lax.dot_general(a, b, (((1,), (1,)), ((), ())), preferred_element_type=F32)


def dot_tn(a, b):
    return lax.dot_general(a, b, (((0,), (0,)), ((), ())), preferred_element_type=F32)


def kernel(
    n_ctx, q_hbm, k_hbm, v_hbm, w_hbm, c_hbm, offs,
    mixed_hbm, dq_hbm, dk_hbm, dv_hbm,
    own_q, own_k, own_v, own_do, w_ref, cot, kv, qo, stats, stats_in,
    att, acc, mix_out, mix_in, out_v,
    load_sem, cot_send, cot_recv, kv_send, kv_recv, qo_send, qo_recv,
    st_send, st_recv, mix_send, mix_recv, out_sem,
):
    rows = q_hbm.shape[0]
    feats = q_hbm.shape[1]
    heads = feats // HD
    scale = 1.0 / math.sqrt(HD)
    scale2 = scale * LOG2E
    me = lax.axis_index("ctx")
    grp = lax.axis_index("head")
    right = lax.rem(me + 1, n_ctx)
    left = lax.rem(me + n_ctx - 1, n_ctx)
    left2 = lax.rem(me + n_ctx - 2, n_ctx)
    right2 = lax.rem(me + 2, n_ctx)
    core = lax.rem(grp, 2)
    pair = grp // 2
    core_mate = pair * 2 + (1 - core)
    x_mate = (1 - pair) * 2 + core
    x_core_mate = (1 - pair) * 2 + (1 - core)

    barrier = pltpu.get_barrier_semaphore()
    for target in ((right, grp), (left, grp), (right2, grp), (me, core_mate), (me, x_mate)):
        pl.semaphore_signal(barrier, inc=1, device_id=target, device_id_type=MESH)

    def cols(ref, h):
        return ref.at[:, h * HD : (h + 1) * HD]

    loads = []
    for slot, (src, dst) in enumerate(((c_hbm, cot.at[0]), (w_hbm, w_ref))):
        loads.append(pltpu.make_async_copy(src, dst, load_sem.at[slot]))
    head_loads = []
    for a, (src, dst) in enumerate(((q_hbm, own_q), (k_hbm, own_k), (v_hbm, own_v))):
        for h in range(heads):
            head_loads.append(
                pltpu.make_async_copy(cols(src, h), dst.at[h], load_sem.at[2 + a * heads + h])
            )
    for copy in loads + head_loads:
        copy.start()

    def remote(src, dst, send, recv, target):
        return pltpu.make_async_remote_copy(
            src_ref=src, dst_ref=dst, send_sem=send, recv_sem=recv,
            device_id=target, device_id_type=MESH,
        )

    def kv_copy(hop, a, h):
        src = cols((k_hbm, v_hbm)[a], h) if hop == 0 else kv.at[0, a, h]
        return remote(
            src, kv.at[hop, a, h], kv_send.at[hop, a, h], kv_recv.at[hop, a, h], (right, grp)
        )

    def qo_copy(hop, a, h):
        if hop == 0:
            src = cols(q_hbm, h) if a == 0 else own_do.at[h]
        else:
            src = qo.at[0, a, h]
        return remote(
            src, qo.at[hop, a, h], qo_send.at[hop, a, h], qo_recv.at[hop, a, h], (left, grp)
        )

    cot_core = remote(c_hbm, cot.at[1], cot_send.at[0], cot_recv.at[0], (me, core_mate))
    cot_x = remote(c_hbm, cot.at[2], cot_send.at[1], cot_recv.at[1], (me, x_mate))
    cot_relay = remote(cot.at[2], cot.at[3], cot_send.at[2], cot_recv.at[2], (me, core_mate))

    pl.semaphore_wait(barrier, 5)
    cot_x.start()
    cot_core.start()
    for h in range(2):
        kv_copy(0, 0, h).start()
        kv_copy(0, 1, h).start()
    for h in range(heads):
        qo_copy(0, 0, h).start()

    base = me * rows
    q_pos = base + lax.broadcasted_iota(jnp.int32, (rows, 128), 0)
    first = jnp.zeros((rows, 128), jnp.int32)
    for g in range(offs.shape[1]):
        starts = jnp.broadcast_to(offs[0, g : g + 1, :], (rows, 128))
        later = jnp.broadcast_to(offs[1, g : g + 1, :], (rows, 128))
        first = jnp.maximum(first, jnp.where(later <= q_pos, starts, 0))
    first = (first - base).astype(F32)
    low = jnp.max(first.T, axis=0, keepdims=True)
    stats[...] = jnp.zeros(stats.shape, F32)
    stats[2 * heads : 2 * heads + 1, :] = low

    def w_block(index):
        return w_ref[:, pl.ds(pl.multiple_of(index * feats, feats), feats)]

    def relay_kv(h):
        for a in range(2):
            kv_copy(0, a, h).wait_recv()
            kv_copy(1, a, h).start()
        if h + 2 < heads:
            for a in range(2):
                kv_copy(0, a, h + 2).start()

    def relay_qo(a, h):
        qo_copy(0, a, h).wait_recv()
        qo_copy(1, a, h).start()

    loads[0].wait()
    loads[1].wait()
    grad = dot_nt(cot[0], w_block(grp))
    cot_core.wait_recv()
    grad += dot_nt(cot[1], w_block(core_mate))
    relay_kv(0)
    cot_x.wait_recv()
    cot_relay.start()
    grad += dot_nt(cot[2], w_block(x_mate))
    relay_kv(1)
    cot_relay.wait_recv()
    grad += dot_nt(cot[3], w_block(x_core_mate))
    for h in range(heads):
        own_do[h] = grad[:, h * HD : (h + 1) * HD].astype(BF16)
        qo_copy(0, 1, h).start()
    for h in range(heads):
        relay_qo(0, h)
    for copy in head_loads:
        copy.wait()

    key_row = lax.broadcasted_iota(jnp.int32, (rows, rows), 0).astype(F32)
    query_col = lax.broadcasted_iota(jnp.int32, (rows, rows), 1).astype(F32)

    def query_side(h):
        query = own_q[h]
        grad_o = own_do[h]
        key_tiles = (own_k[h], kv[0, 0, h], kv[1, 0, h])
        value_tiles = (own_v[h], kv[0, 1, h], kv[1, 1, h])
        scores = []
        for d in range(3):
            mask = key_row >= low + float(d * rows)
            if d == 0:
                mask = mask & (key_row <= query_col)
            raw = dot_nt(key_tiles[d], query) * scale2
            scores.append(jnp.where(mask, raw, NEG_FILL))
        top = functools.reduce(jnp.maximum, [jnp.max(s, axis=0, keepdims=True) for s in scores])
        expd = [jnp.exp2(s - top) for s in scores]
        total = functools.reduce(jnp.add, [jnp.sum(e, axis=0, keepdims=True) for e in expd])
        inverse = 1.0 / total
        probs = [e * inverse for e in expd]
        probs_b = [p.astype(BF16) for p in probs]
        mixed_t = sum(dot_tn(value_tiles[d], probs_b[d]) for d in range(3))
        attended = mixed_t.T.astype(BF16)
        att[:, h * HD : (h + 1) * HD] = attended
        product = grad_o.astype(F32) * attended.astype(F32)
        delta = jnp.sum(product.T, axis=0, keepdims=True)
        stats[h : h + 1, :] = top + jnp.log2(total)
        stats[heads + h : heads + h + 1, :] = delta
        grads_b = []
        for d in range(3):
            grad_p = dot_nt(value_tiles[d], grad_o)
            grads_b.append((scale * probs[d] * (grad_p - delta)).astype(BF16))
        dq_t = sum(dot_tn(key_tiles[d], grads_b[d]) for d in range(3))
        out_v[0, :, h * HD : (h + 1) * HD] = dq_t.T.astype(BF16)
        acc[0, h] = dot_nn(grads_b[0], query)
        acc[1, h] = dot_nn(probs_b[0], grad_o)

    def key_side(h):
        grad_k = acc[0, h]
        grad_v = acc[1, h]
        for d in range(2):
            query = qo[d, 0, h]
            grad_o = qo[d, 1, h]
            far_low = stats_in[d, 2 * heads : 2 * heads + 1, :] + float((d + 1) * rows)
            log_total = stats_in[d, h : h + 1, :]
            delta = stats_in[d, heads + h : heads + h + 1, :]
            raw = dot_nt(own_k[h], query) * scale2
            probs = jnp.where(key_row >= far_low, jnp.exp2(raw - log_total), 0.0)
            grad_v += dot_nn(probs.astype(BF16), grad_o)
            grad_p = dot_nt(own_v[h], grad_o)
            grad_k += dot_nn((scale * probs * (grad_p - delta)).astype(BF16), query)
        out_v[1, :, h * HD : (h + 1) * HD] = grad_k.astype(BF16)
        out_v[2, :, h * HD : (h + 1) * HD] = grad_v.astype(BF16)

    def wait_far_kv(h):
        for a in range(2):
            kv_copy(1, a, h).wait_recv()

    relay_kv(2)
    wait_far_kv(0)
    query_side(0)
    relay_kv(3)
    relay_qo(1, 0)
    wait_far_kv(1)
    query_side(1)
    relay_qo(1, 1)
    relay_qo(1, 2)
    wait_far_kv(2)
    query_side(2)
    relay_qo(1, 3)
    wait_far_kv(3)
    query_side(3)

    stat_copies = [
        remote(stats, stats_in.at[d], st_send.at[d], st_recv.at[d], (target, grp))
        for d, target in enumerate((left, left2))
    ]
    for copy in stat_copies:
        copy.start()
    out_dq = pltpu.make_async_copy(out_v.at[0], dq_hbm, out_sem.at[0])
    out_dq.start()

    mix_a = remote(mix_out.at[0], mix_in.at[0], mix_send.at[0], mix_recv.at[0], (me, core_mate))
    mix_c = remote(mix_out.at[1], mix_in.at[1], mix_send.at[1], mix_recv.at[1], (me, core_mate))
    mix_x = remote(mix_out.at[2], mix_in.at[2], mix_send.at[2], mix_recv.at[2], (me, x_mate))
    mix_out[0] = dot_nn(att[...], w_block(x_core_mate)).astype(BF16)
    mix_a.start()
    far_part = dot_nn(att[...], w_block(x_mate))
    mix_a.wait_recv()
    mix_out[2] = (far_part + mix_in[0].astype(F32)).astype(BF16)
    mix_x.start()
    mix_out[1] = dot_nn(att[...], w_block(core_mate)).astype(BF16)
    mix_c.start()

    for copy in stat_copies:
        copy.wait_recv()
    for h in range(heads):
        qo_copy(1, 0, h).wait_recv()
        qo_copy(1, 1, h).wait_recv()
        key_side(h)
    out_dk = pltpu.make_async_copy(out_v.at[1], dk_hbm, out_sem.at[1])
    out_dv = pltpu.make_async_copy(out_v.at[2], dv_hbm, out_sem.at[2])
    out_dk.start()
    out_dv.start()

    own_part = dot_nn(att[...], w_block(grp))
    mix_c.wait_recv()
    own_part += mix_in[1].astype(F32)
    mix_x.wait_recv()
    out_v[3] = (own_part + mix_in[2].astype(F32)).astype(BF16)
    out_mixed = pltpu.make_async_copy(out_v.at[3], mixed_hbm, out_sem.at[3])
    out_mixed.start()

    cot_core.wait_send()
    cot_x.wait_send()
    cot_relay.wait_send()
    for hop in range(2):
        for a in range(2):
            for h in range(heads):
                kv_copy(hop, a, h).wait_send()
                qo_copy(hop, a, h).wait_send()
    for copy in stat_copies + [mix_a, mix_c, mix_x]:
        copy.wait_send()
    for copy in (out_dq, out_dk, out_dv, out_mixed):
        copy.wait()


def per_device(n_ctx, queries, key_rows, value_rows, out_weight, cotangent, offsets):
    rows, feats = queries.shape
    heads = feats // HD
    count = offsets.shape[0]
    groups = -(-count // 128)
    later = jnp.concatenate(
        [offsets[PREV:], jnp.full((groups * 128 - count + PREV,), 2**30, jnp.int32)]
    )
    starts = jnp.concatenate([offsets, jnp.zeros((groups * 128 - count,), jnp.int32)])
    offs = jnp.stack([starts, later]).reshape(2, groups, 128)
    any_spec = pl.BlockSpec(memory_space=pl.ANY)
    tile = jax.ShapeDtypeStruct((rows, feats), BF16)
    dma = pltpu.SemaphoreType.DMA
    outs = pl.pallas_call(
        functools.partial(kernel, n_ctx),
        out_shape=(tile, tile, tile, tile),
        in_specs=[any_spec] * 5 + [pl.BlockSpec(memory_space=pltpu.VMEM)],
        out_specs=(any_spec,) * 4,
        scratch_shapes=[
            pltpu.VMEM((heads, rows, HD), BF16),
            pltpu.VMEM((heads, rows, HD), BF16),
            pltpu.VMEM((heads, rows, HD), BF16),
            pltpu.VMEM((heads, rows, HD), BF16),
            pltpu.VMEM(out_weight.shape, BF16),
            pltpu.VMEM((4, rows, feats), BF16),
            pltpu.VMEM((2, 2, heads, rows, HD), BF16),
            pltpu.VMEM((2, 2, heads, rows, HD), BF16),
            pltpu.VMEM((16, rows), F32),
            pltpu.VMEM((2, 16, rows), F32),
            pltpu.VMEM((rows, feats), BF16),
            pltpu.VMEM((2, heads, rows, HD), F32),
            pltpu.VMEM((3, rows, feats), BF16),
            pltpu.VMEM((3, rows, feats), BF16),
            pltpu.VMEM((4, rows, feats), BF16),
            dma((2 + 3 * heads,)),
            dma((3,)),
            dma((3,)),
            dma((2, 2, heads)),
            dma((2, 2, heads)),
            dma((2, 2, heads)),
            dma((2, 2, heads)),
            dma((2,)),
            dma((2,)),
            dma((3,)),
            dma((3,)),
            dma((4,)),
        ],
        compiler_params=pltpu.CompilerParams(
            collective_id=0, has_side_effects=True, vmem_limit_bytes=48 * 1024 * 1024
        ),
    )(queries, key_rows, value_rows, out_weight, cotangent, offs)
    return outs


def solution(mesh):
    in_specs = (
        P("ctx", "head"),
        P("ctx", "head"),
        P("ctx", "head"),
        P("head", None),
        P("ctx", "head"),
        P(),
    )
    out_specs = (P("ctx", "head"), P("ctx", "head"), P("ctx", "head"), P("ctx", "head"))
    return jax.shard_map(
        functools.partial(per_device, mesh.shape["ctx"]),
        mesh=mesh,
        in_specs=in_specs,
        out_specs=out_specs,
        check_vma=False,
    )
```

time: 197 us -> 98.3 us (0.50)
  the two profiles are of different devices: /device:TPU:483 before, /device:TPU:465 now
where the time goes in v1:
time: 98.3 us; the launch traced here: 97.9 us
  Pallas kernels  87.2 us (89%)
  local copies, waits for them, and re-layouts  10 us (10%)
    pallas_call x1, Pallas kernels, per_device(): pl.pallas_call(functools.partial(kernel, n_ctx), out_shape=(tile, tile, t...  87.2 us
    unnamed x14, local copies, waits for them, and re-layouts  8.55 us

profile of v1, /device:TPU:465, one launch (start us, length us, event | category | flops | bytes accessed | tf_op | source)
XLA Modules:
  0.0 97.9 jit_solution(1919815664308371602)
XLA Ops:
  0.6 0.8 slice.3
  1.4 0.7 pad_bitcast_fusion
  2.1 0.0 copy-start
  2.1 1.6 %copy-done = bf16[512,2048]{1,0:T(8,128)(2,1)S(1)} copy-done((bf16[512,2048]{1,0:T(8,128)(2,1)S(1)}, bf16[512,2048]{1,0:T(8,128)(2,1)}, u32[]{:S(2)}) %copy-start) | copy-done | bytes 2097176
  3.7 0.0 copy-start.1
  3.7 1.0 %copy-done.1 = bf16[384,512]{1,0:T(8,128)(2,1)S(1)} copy-done((bf16[384,512]{1,0:T(8,128)(2,1)S(1)}, bf16[384,512]{1,0:T(8,128)(2,1)}, u32[]{:S(2)}) %copy-start.1) | copy-done | bytes 393240
  4.7 0.0 copy-start.2
  4.7 1.0 %copy-done.2 = bf16[384,512]{1,0:T(8,128)(2,1)S(1)} copy-done((bf16[384,512]{1,0:T(8,128)(2,1)S(1)}, bf16[384,512]{1,0:T(8,128)(2,1)}, u32[]{:S(2)}) %copy-start.2) | copy-done | bytes 393240
  5.7 0.0 copy-start.3
  5.7 1.0 %copy-done.3 = bf16[384,512]{1,0:T(8,128)(2,1)S(1)} copy-done((bf16[384,512]{1,0:T(8,128)(2,1)S(1)}, bf16[384,512]{1,0:T(8,128)(2,1)}, u32[]{:S(2)}) %copy-start.3) | copy-done | bytes 393240
  6.7 0.0 copy-start.4
  6.7 1.0 %copy-done.4 = bf16[384,512]{1,0:T(8,128)(2,1)S(1)} copy-done((bf16[384,512]{1,0:T(8,128)(2,1)S(1)}, bf16[384,512]{1,0:T(8,128)(2,1)}, u32[]{:S(2)}) %copy-start.4) | copy-done | bytes 393240
  7.7 87.2 %shard_map.93 = (bf16[384,512]{1,0:T(8,128)(2,1)S(1)}, bf16[384,512]{1,0:T(8,128)(2,1)S(1)}, bf16[384,512]{1,0:T(8,128)(2,1)S(1)}, bf16[384,512]{1,0:T(8,128)(2,1)S(1)}) custom-call(bf16[384,512]{1,0:T(8,128)(2,1)S(1)} %copy-done.1, bf16[384,512]{1,0:T(8,128)(2,1)S(1)} %copy-done.2, bf16[384,512]{1,0:T(8,128)(2,1)S(1)} %copy-done.3, ...), custom_call_target="tpu_custom_call" | custom-call | tf_op jit(solution)/shard_map/pallas_call | solution.py:297
  94.9 0.7 copy.14
  95.7 0.7 copy.15
  96.4 0.7 copy.16
  97.2 0.7 copy.17
  (1 shorter events, 0.0 us)
Async XLA Ops:
  2.1 1.6 %copy-start = (bf16[512,2048]{1,0:T(8,128)(2,1)S(1)}, bf16[512,2048]{1,0:T(8,128)(2,1)}, u32[]{:S(2)}) copy-start(bf16[512,2048]{1,0:T(8,128)(2,1)} %w_hbm.1) | copy-start | bytes 6291460
  3.7 1.0 %copy-start.1 = (bf16[384,512]{1,0:T(8,128)(2,1)S(1)}, bf16[384,512]{1,0:T(8,128)(2,1)}, u32[]{:S(2)}) copy-start(bf16[384,512]{1,0:T(8,128)(2,1)} %q_hbm.1) | copy-start | bytes 1179652
  4.7 1.0 %copy-start.2 = (bf16[384,512]{1,0:T(8,128)(2,1)S(1)}, bf16[384,512]{1,0:T(8,128)(2,1)}, u32[]{:S(2)}) copy-start(bf16[384,512]{1,0:T(8,128)(2,1)} %k_hbm.1) | copy-start | bytes 1179652
  5.7 1.0 %copy-start.3 = (bf16[384,512]{1,0:T(8,128)(2,1)S(1)}, bf16[384,512]{1,0:T(8,128)(2,1)}, u32[]{:S(2)}) copy-start(bf16[384,512]{1,0:T(8,128)(2,1)} %v_hbm.1) | copy-start | bytes 1179652
  6.7 1.0 %copy-start.4 = (bf16[384,512]{1,0:T(8,128)(2,1)S(1)}, bf16[384,512]{1,0:T(8,128)(2,1)}, u32[]{:S(2)}) copy-start(bf16[384,512]{1,0:T(8,128)(2,1)} %c_hbm.1) | copy-start | bytes 1179652

commit v2 on v1

--- a/solution.py
+++ b/solution.py
@@ -30,24 +30,35 @@
 
 
 def kernel(
-    n_ctx, q_hbm, k_hbm, v_hbm, w_hbm, c_hbm, offs,
-    mixed_hbm, dq_hbm, dk_hbm, dv_hbm,
+    n_ctx, groups, q_hbm, k_hbm, v_hbm, w_hbm, c_hbm, offs,
+    out_ref,
     own_q, own_k, own_v, own_do, w_ref, cot, kv, qo, stats, stats_in,
-    att, acc, mix_out, mix_in, out_v,
+    att, acc, mix_out, mix_in,
     load_sem, cot_send, cot_recv, kv_send, kv_recv, qo_send, qo_recv,
-    st_send, st_recv, mix_send, mix_recv, out_sem,
+    st_send, st_recv, mix_send, mix_recv,
 ):
     rows = q_hbm.shape[0]
     feats = q_hbm.shape[1]
     heads = feats // HD
     scale = 1.0 / math.sqrt(HD)
     scale2 = scale * LOG2E
+    half = n_ctx // 2
     me = lax.axis_index("ctx")
     grp = lax.axis_index("head")
-    right = lax.rem(me + 1, n_ctx)
-    left = lax.rem(me + n_ctx - 1, n_ctx)
-    left2 = lax.rem(me + n_ctx - 2, n_ctx)
-    right2 = lax.rem(me + 2, n_ctx)
+    first_dev = me == 0
+    last_dev = me == n_ctx - 1
+    at_end = (me == half - 1).astype(jnp.int32)
+    at_start = (me == half).astype(jnp.int32)
+    is_last = last_dev.astype(jnp.int32)
+    is_first = first_dev.astype(jnp.int32)
+    right = me + 1 + at_end * (n_ctx - 1 - half) + is_last * (half - n_ctx)
+    left = me - 1 + at_start * (1 - half) + is_first * half
+    from_left = me - 1 + at_start * half + is_first * (half + 1)
+    from_right = me + 1 - at_end * half + is_last * (half - 1 - n_ctx)
+    to_stats = lax.rem(me + n_ctx - 1, n_ctx)
+    to_stats2 = lax.rem(me + n_ctx - 2, n_ctx)
+    of_stats = lax.rem(me + 1, n_ctx)
+    of_stats2 = lax.rem(me + 2, n_ctx)
     core = lax.rem(grp, 2)
     pair = grp // 2
     core_mate = pair * 2 + (1 - core)
@@ -55,7 +66,11 @@
     x_core_mate = (1 - pair) * 2 + (1 - core)
 
     barrier = pltpu.get_barrier_semaphore()
-    for target in ((right, grp), (left, grp), (right2, grp), (me, core_mate), (me, x_mate)):
+    senders = (
+        (from_left, grp), (from_right, grp), (of_stats, grp), (of_stats2, grp),
+        (me, core_mate), (me, x_mate),
+    )
+    for target in senders:
         pl.semaphore_signal(barrier, inc=1, device_id=target, device_id_type=MESH)
 
     def cols(ref, h):
@@ -79,40 +94,124 @@
             device_id=target, device_id_type=MESH,
         )
 
-    def kv_copy(hop, a, h):
-        src = cols((k_hbm, v_hbm)[a], h) if hop == 0 else kv.at[0, a, h]
+    def kv_copy(hop, a, h, src=None):
+        slot = hop + 2 * at_end
         return remote(
-            src, kv.at[hop, a, h], kv_send.at[hop, a, h], kv_recv.at[hop, a, h], (right, grp)
+            kv.at[0, a, h] if src is None else src, kv.at[slot, a, h],
+            kv_send.at[hop, a, h], kv_recv.at[slot, a, h], (right, grp),
         )
 
-    def qo_copy(hop, a, h):
-        if hop == 0:
-            src = cols(q_hbm, h) if a == 0 else own_do.at[h]
-        else:
-            src = qo.at[0, a, h]
+    def qo_copy(hop, a, h, src=None):
+        slot = hop + 2 * at_start
         return remote(
-            src, qo.at[hop, a, h], qo_send.at[hop, a, h], qo_recv.at[hop, a, h], (left, grp)
+            qo.at[0, a, h] if src is None else src, qo.at[slot, a, h],
+            qo_send.at[hop, a, h], qo_recv.at[slot, a, h], (left, grp),
         )
+
+    def arrived(buf, sems, slot, a, h):
+        part, sem = buf.at[slot, a, h], sems.at[slot, a, h]
+        remote(part, part, sem, sem, (me, core_mate)).wait_recv()
+
+    def send_own_kv(h):
+        @pl.when(jnp.logical_not(last_dev))
+        def _():
+            kv_copy(0, 0, h, cols(k_hbm, h)).start()
+            kv_copy(0, 1, h, cols(v_hbm, h)).start()
+
+    def send_own_qo(a, h):
+        @pl.when(jnp.logical_not(first_dev))
+        def _():
+            qo_copy(0, a, h, cols(q_hbm, h) if a == 0 else own_do.at[h]).start()
+
+    def relay_kv(h):
+        for a in range(2):
+            @pl.when(jnp.logical_not(first_dev))
+            def _():
+                arrived(kv, kv_recv, 0, a, h)
+
+            @pl.when((me > 0) & (me < n_ctx - 1))
+            def _():
+                kv_copy(1, a, h).start()
+
+            @pl.when(last_dev)
+            def _():
+                arrived(kv, kv_recv, 2, a, h)
+                kv_copy(0, a, h, kv.at[2, a, h]).start()
+
+    def wait_far_kv(h):
+        for a in range(2):
+            @pl.when(me > 1)
+            def _():
+                arrived(kv, kv_recv, 1, a, h)
+
+            @pl.when(last_dev)
+            def _():
+                arrived(kv, kv_recv, 3, a, h)
+                kv_copy(1, a, h, kv.at[3, a, h]).start()
+
+    def relay_qo(a, h):
+        @pl.when(jnp.logical_not(last_dev))
+        def _():
+            arrived(qo, qo_recv, 0, a, h)
+
+        @pl.when((me > 0) & (me < n_ctx - 1))
+        def _():
+            qo_copy(1, a, h).start()
+
+        @pl.when(first_dev)
+        def _():
+            arrived(qo, qo_recv, 2, a, h)
+            qo_copy(0, a, h, qo.at[2, a, h]).start()
+
+    def forward_far_qo(a, h):
+        @pl.when(first_dev)
+        def _():
+            arrived(qo, qo_recv, 3, a, h)
+            qo_copy(1, a, h, qo.at[3, a, h]).start()
+
+    def wait_far_qo(h):
+        for a in range(2):
+            @pl.when(me < n_ctx - 2)
+            def _():
+                arrived(qo, qo_recv, 1, a, h)
 
     cot_core = remote(c_hbm, cot.at[1], cot_send.at[0], cot_recv.at[0], (me, core_mate))
     cot_x = remote(c_hbm, cot.at[2], cot_send.at[1], cot_recv.at[1], (me, x_mate))
     cot_relay = remote(cot.at[2], cot.at[3], cot_send.at[2], cot_recv.at[2], (me, core_mate))
 
-    pl.semaphore_wait(barrier, 5)
+    pl.semaphore_wait(barrier, 6)
     cot_x.start()
     cot_core.start()
-    for h in range(2):
-        kv_copy(0, 0, h).start()
-        kv_copy(0, 1, h).start()
     for h in range(heads):
-        qo_copy(0, 0, h).start()
+        send_own_qo(0, h)
+        send_own_kv(h)
+
+    @pl.when(first_dev)
+    def _():
+        kv[0] = jnp.zeros(kv.shape[1:], BF16)
+
+    @pl.when(me <= 1)
+    def _():
+        kv[1] = jnp.zeros(kv.shape[1:], BF16)
+
+    @pl.when(last_dev)
+    def _():
+        qo[0] = jnp.zeros(qo.shape[1:], BF16)
+
+    @pl.when(me >= n_ctx - 2)
+    def _():
+        qo[1] = jnp.zeros(qo.shape[1:], BF16)
 
     base = me * rows
     q_pos = base + lax.broadcasted_iota(jnp.int32, (rows, 128), 0)
     first = jnp.zeros((rows, 128), jnp.int32)
-    for g in range(offs.shape[1]):
-        starts = jnp.broadcast_to(offs[0, g : g + 1, :], (rows, 128))
-        later = jnp.broadcast_to(offs[1, g : g + 1, :], (rows, 128))
+    lists = offs[...]
+    turned = pltpu.roll(lists, 128 - PREV, 1)
+    lane = lax.broadcasted_iota(jnp.int32, lists.shape, 1)
+    ahead = jnp.where(lane < 128 - PREV, turned, pltpu.roll(turned, lists.shape[0] - 1, 0))
+    for g in range(groups):
+        starts = jnp.broadcast_to(lists[g : g + 1, :], (rows, 128))
+        later = jnp.broadcast_to(ahead[g : g + 1, :], (rows, 128))
         first = jnp.maximum(first, jnp.where(later <= q_pos, starts, 0))
     first = (first - base).astype(F32)
     low = jnp.max(first.T, axis=0, keepdims=True)
@@ -122,23 +221,13 @@
     def w_block(index):
         return w_ref[:, pl.ds(pl.multiple_of(index * feats, feats), feats)]
 
-    def relay_kv(h):
-        for a in range(2):
-            kv_copy(0, a, h).wait_recv()
-            kv_copy(1, a, h).start()
-        if h + 2 < heads:
-            for a in range(2):
-                kv_copy(0, a, h + 2).start()
-
-    def relay_qo(a, h):
-        qo_copy(0, a, h).wait_recv()
-        qo_copy(1, a, h).start()
-
     loads[0].wait()
     loads[1].wait()
     grad = dot_nt(cot[0], w_block(grp))
     cot_core.wait_recv()
     grad += dot_nt(cot[1], w_block(core_mate))
+    for h in range(heads):
+        relay_qo(0, h)
     relay_kv(0)
     cot_x.wait_recv()
     cot_relay.start()
@@ -148,9 +237,7 @@
     grad += dot_nt(cot[3], w_block(x_core_mate))
     for h in range(heads):
         own_do[h] = grad[:, h * HD : (h + 1) * HD].astype(BF16)
-        qo_copy(0, 1, h).start()
-    for h in range(heads):
-        relay_qo(0, h)
+        send_own_qo(1, h)
     for copy in head_loads:
         copy.wait()
 
@@ -187,7 +274,7 @@
             grad_p = dot_nt(value_tiles[d], grad_o)
             grads_b.append((scale * probs[d] * (grad_p - delta)).astype(BF16))
         dq_t = sum(dot_tn(key_tiles[d], grads_b[d]) for d in range(3))
-        out_v[0, :, h * HD : (h + 1) * HD] = dq_t.T.astype(BF16)
+        out_ref[1, :, h * HD : (h + 1) * HD] = dq_t.T.astype(BF16)
         acc[0, h] = dot_nn(grads_b[0], query)
         acc[1, h] = dot_nn(probs_b[0], grad_o)
 
@@ -205,36 +292,36 @@
             grad_v += dot_nn(probs.astype(BF16), grad_o)
             grad_p = dot_nt(own_v[h], grad_o)
             grad_k += dot_nn((scale * probs * (grad_p - delta)).astype(BF16), query)
-        out_v[1, :, h * HD : (h + 1) * HD] = grad_k.astype(BF16)
-        out_v[2, :, h * HD : (h + 1) * HD] = grad_v.astype(BF16)
-
-    def wait_far_kv(h):
-        for a in range(2):
-            kv_copy(1, a, h).wait_recv()
+        out_ref[2, :, h * HD : (h + 1) * HD] = grad_k.astype(BF16)
+        out_ref[3, :, h * HD : (h + 1) * HD] = grad_v.astype(BF16)
 
     relay_kv(2)
+    for h in range(heads):
+        forward_far_qo(0, h)
+    relay_kv(3)
     wait_far_kv(0)
     query_side(0)
-    relay_kv(3)
     relay_qo(1, 0)
+    relay_qo(1, 1)
     wait_far_kv(1)
+    forward_far_qo(1, 0)
     query_side(1)
-    relay_qo(1, 1)
     relay_qo(1, 2)
+    relay_qo(1, 3)
     wait_far_kv(2)
+    forward_far_qo(1, 1)
     query_side(2)
-    relay_qo(1, 3)
     wait_far_kv(3)
+    forward_far_qo(1, 2)
     query_side(3)
+    forward_far_qo(1, 3)
 
     stat_copies = [
         remote(stats, stats_in.at[d], st_send.at[d], st_recv.at[d], (target, grp))
-        for d, target in enumerate((left, left2))
+        for d, target in enumerate((to_stats, to_stats2))
     ]
     for copy in stat_copies:
         copy.start()
-    out_dq = pltpu.make_async_copy(out_v.at[0], dq_hbm, out_sem.at[0])
-    out_dq.start()
 
     mix_a = remote(mix_out.at[0], mix_in.at[0], mix_send.at[0], mix_recv.at[0], (me, core_mate))
     mix_c = remote(mix_out.at[1], mix_in.at[1], mix_send.at[1], mix_recv.at[1], (me, core_mate))
@@ -251,33 +338,42 @@
     for copy in stat_copies:
         copy.wait_recv()
     for h in range(heads):
-        qo_copy(1, 0, h).wait_recv()
-        qo_copy(1, 1, h).wait_recv()
+        wait_far_qo(h)
         key_side(h)
-    out_dk = pltpu.make_async_copy(out_v.at[1], dk_hbm, out_sem.at[1])
-    out_dv = pltpu.make_async_copy(out_v.at[2], dv_hbm, out_sem.at[2])
-    out_dk.start()
-    out_dv.start()
 
     own_part = dot_nn(att[...], w_block(grp))
     mix_c.wait_recv()
     own_part += mix_in[1].astype(F32)
     mix_x.wait_recv()
-    out_v[3] = (own_part + mix_in[2].astype(F32)).astype(BF16)
-    out_mixed = pltpu.make_async_copy(out_v.at[3], mixed_hbm, out_sem.at[3])
-    out_mixed.start()
+    out_ref[0] = (own_part + mix_in[2].astype(F32)).astype(BF16)
 
     cot_core.wait_send()
     cot_x.wait_send()
     cot_relay.wait_send()
-    for hop in range(2):
-        for a in range(2):
-            for h in range(heads):
-                kv_copy(hop, a, h).wait_send()
-                qo_copy(hop, a, h).wait_send()
+    for a in range(2):
+        for h in range(heads):
+            kv_copy(0, a, h).wait_send()
+            qo_copy(0, a, h).wait_send()
+
+            @pl.when(jnp.logical_not(first_dev))
+            def _():
+                kv_copy(1, a, h).wait_send()
+
+            @pl.when(jnp.logical_not(last_dev))
+            def _():
+                qo_copy(1, a, h).wait_send()
     for copy in stat_copies + [mix_a, mix_c, mix_x]:
         copy.wait_send()
-    for copy in (out_dq, out_dk, out_dv, out_mixed):
+
+
+def spread(all_ref, *refs):
+    outs, sems = refs[:-1], refs[-1]
+    copies = [
+        pltpu.make_async_copy(all_ref.at[i], out, sems.at[i]) for i, out in enumerate(outs)
+    ]
+    for copy in copies:
+        copy.start()
+    for copy in copies:
         copy.wait()
 
 
@@ -286,19 +382,18 @@
     heads = feats // HD
     count = offsets.shape[0]
     groups = -(-count // 128)
-    later = jnp.concatenate(
-        [offsets[PREV:], jnp.full((groups * 128 - count + PREV,), 2**30, jnp.int32)]
-    )
-    starts = jnp.concatenate([offsets, jnp.zeros((groups * 128 - count,), jnp.int32)])
-    offs = jnp.stack([starts, later]).reshape(2, groups, 128)
+    padded = -(-(groups + 1) // 8) * 8
+    offs = jnp.pad(offsets, (0, padded * 128 - count), constant_values=2**30)
+    offs = offs.reshape(padded, 128)
     any_spec = pl.BlockSpec(memory_space=pl.ANY)
+    vmem_spec = pl.BlockSpec(memory_space=pltpu.VMEM)
     tile = jax.ShapeDtypeStruct((rows, feats), BF16)
     dma = pltpu.SemaphoreType.DMA
-    outs = pl.pallas_call(
-        functools.partial(kernel, n_ctx),
-        out_shape=(tile, tile, tile, tile),
-        in_specs=[any_spec] * 5 + [pl.BlockSpec(memory_space=pltpu.VMEM)],
-        out_specs=(any_spec,) * 4,
+    four = pl.pallas_call(
+        functools.partial(kernel, n_ctx, groups),
+        out_shape=jax.ShapeDtypeStruct((4, rows, feats), BF16),
+        in_specs=[any_spec] * 5 + [vmem_spec],
+        out_specs=vmem_spec,
         scratch_shapes=[
             pltpu.VMEM((heads, rows, HD), BF16),
             pltpu.VMEM((heads, rows, HD), BF16),
@@ -306,33 +401,37 @@
             pltpu.VMEM((heads, rows, HD), BF16),
             pltpu.VMEM(out_weight.shape, BF16),
             pltpu.VMEM((4, rows, feats), BF16),
-            pltpu.VMEM((2, 2, heads, rows, HD), BF16),
-            pltpu.VMEM((2, 2, heads, rows, HD), BF16),
+            pltpu.VMEM((4, 2, heads, rows, HD), BF16),
+            pltpu.VMEM((4, 2, heads, rows, HD), BF16),
             pltpu.VMEM((16, rows), F32),
             pltpu.VMEM((2, 16, rows), F32),
             pltpu.VMEM((rows, feats), BF16),
             pltpu.VMEM((2, heads, rows, HD), F32),
             pltpu.VMEM((3, rows, feats), BF16),
             pltpu.VMEM((3, rows, feats), BF16),
-            pltpu.VMEM((4, rows, feats), BF16),
             dma((2 + 3 * heads,)),
             dma((3,)),
             dma((3,)),
             dma((2, 2, heads)),
+            dma((4, 2, heads)),
             dma((2, 2, heads)),
-            dma((2, 2, heads)),
-            dma((2, 2, heads)),
+            dma((4, 2, heads)),
             dma((2,)),
             dma((2,)),
             dma((3,)),
             dma((3,)),
-            dma((4,)),
         ],
         compiler_params=pltpu.CompilerParams(
-            collective_id=0, has_side_effects=True, vmem_limit_bytes=48 * 1024 * 1024
+            collective_id=0, has_side_effects=True, vmem_limit_bytes=58 * 1024 * 1024
         ),
     )(queries, key_rows, value_rows, out_weight, cotangent, offs)
-    return outs
+    return pl.pallas_call(
+        spread,
+        out_shape=(tile,) * 4,
+        in_specs=[any_spec],
+        out_specs=(any_spec,) * 4,
+        scratch_shapes=[dma((4,))],
+    )(four)
 
 
 def solution(mesh):

time: 98.3 us -> 132 us (1.34)
  the two profiles are of different devices: /device:TPU:465 before, /device:TPU:1 now
where the time goes in v2:
time: 132 us
  Pallas kernels  130 us (98%)
    pallas_call x1, Pallas kernels, per_device(): pl.pallas_call(functools.partial(kernel, n_ctx, groups), out_shape=jax.Sh...  81.5 us
    pallas_call x1, Pallas kernels, per_device(): pl.pallas_call(spread, out_shape=(tile,) * 4, in_specs=[any_spec], out_sp...  48.8 us

profile of v2, /device:TPU:1, one launch (start us, length us, event | category | flops | bytes accessed | tf_op | source)
XLA Modules:
  0.0 132.3 jit_solution(966649762041249787)
XLA Ops:
  0.6 1.3 pad_bitcast_fusion.offs
  1.9 81.5 %shard_map.93.all_ref = bf16[4,384,512]{2,1,0:T(8,128)(2,1)} custom-call(bf16[384,512]{1,0:T(8,128)(2,1)} %q_hbm.1, bf16[384,512]{1,0:T(8,128)(2,1)} %k_hbm.1, bf16[384,512]{1,0:T(8,128)(2,1)} %v_hbm.1, bf16[512,2048]{1,0:T(8,128)(2,1)} %w_hbm.1, bf16[384,512]{1,0:T(8,128)(2,1)} %c_hbm.1, s32[24,128]{1,0:T(8,128)} %pad_bitcast_fusion.offs), custom_call_target="tpu_custom_call" | custom-call | tf_op jit(solution)/shard_map/pallas_call | solution.py:392
  83.5 48.8 %shard_map.94 = (bf16[384,512]{1,0:T(8,128)(2,1)}, bf16[384,512]{1,0:T(8,128)(2,1)}, bf16[384,512]{1,0:T(8,128)(2,1)}, bf16[384,512]{1,0:T(8,128)(2,1)}) custom-call(bf16[4,384,512]{2,1,0:T(8,128)(2,1)} %shard_map.93.all_ref), custom_call_target="tpu_custom_call" | custom-call | tf_op jit(solution)/shard_map/pallas_call | solution.py:428

commit v3 on v2

--- a/solution.py
+++ b/solution.py
@@ -47,14 +47,16 @@
     grp = lax.axis_index("head")
     first_dev = me == 0
     last_dev = me == n_ctx - 1
-    at_end = (me == half - 1).astype(jnp.int32)
-    at_start = (me == half).astype(jnp.int32)
+    end_dev = me == half - 1
+    start_dev = me == half
+    at_end = end_dev.astype(jnp.int32)
+    at_start = start_dev.astype(jnp.int32)
     is_last = last_dev.astype(jnp.int32)
     is_first = first_dev.astype(jnp.int32)
-    right = me + 1 + at_end * (n_ctx - 1 - half) + is_last * (half - n_ctx)
-    left = me - 1 + at_start * (1 - half) + is_first * half
-    from_left = me - 1 + at_start * half + is_first * (half + 1)
-    from_right = me + 1 - at_end * half + is_last * (half - 1 - n_ctx)
+    key_right = me + 1 + at_end * (n_ctx - 1 - half) + is_last * (half - n_ctx)
+    query_left = me - 1 + at_start * (1 - half) + is_first * half
+    greet_left = me - 1 + is_first * (half + 1)
+    greet_right = me + 1 + is_last * (half - 1 - n_ctx)
     to_stats = lax.rem(me + n_ctx - 1, n_ctx)
     to_stats2 = lax.rem(me + n_ctx - 2, n_ctx)
     of_stats = lax.rem(me + 1, n_ctx)
@@ -67,11 +69,19 @@
 
     barrier = pltpu.get_barrier_semaphore()
     senders = (
-        (from_left, grp), (from_right, grp), (of_stats, grp), (of_stats2, grp),
+        (greet_left, grp), (greet_right, grp), (of_stats, grp), (of_stats2, grp),
         (me, core_mate), (me, x_mate),
     )
     for target in senders:
         pl.semaphore_signal(barrier, inc=1, device_id=target, device_id_type=MESH)
+
+    @pl.when(end_dev)
+    def _():
+        pl.semaphore_signal(barrier, inc=1, device_id=(0, grp), device_id_type=MESH)
+
+    @pl.when(start_dev)
+    def _():
+        pl.semaphore_signal(barrier, inc=1, device_id=(n_ctx - 1, grp), device_id_type=MESH)
 
     def cols(ref, h):
         return ref.at[:, h * HD : (h + 1) * HD]
@@ -95,48 +105,49 @@
         )
 
     def kv_copy(hop, a, h, src=None):
-        slot = hop + 2 * at_end
+        slot = hop + 2 * at_end if a == 0 else hop
         return remote(
             kv.at[0, a, h] if src is None else src, kv.at[slot, a, h],
-            kv_send.at[hop, a, h], kv_recv.at[slot, a, h], (right, grp),
+            kv_send.at[hop, a, h], kv_recv.at[slot, a, h],
+            (key_right if a == 0 else me + 1, grp),
         )
 
     def qo_copy(hop, a, h, src=None):
-        slot = hop + 2 * at_start
+        slot = hop + 2 * at_start if a == 0 else hop
         return remote(
             qo.at[0, a, h] if src is None else src, qo.at[slot, a, h],
-            qo_send.at[hop, a, h], qo_recv.at[slot, a, h], (left, grp),
+            qo_send.at[hop, a, h], qo_recv.at[slot, a, h],
+            (query_left if a == 0 else me - 1, grp),
         )
 
     def arrived(buf, sems, slot, a, h):
         part, sem = buf.at[slot, a, h], sems.at[slot, a, h]
         remote(part, part, sem, sem, (me, core_mate)).wait_recv()
 
+    not_first = jnp.logical_not(first_dev)
+    not_last = jnp.logical_not(last_dev)
+    inner = (me > 0) & (me < n_ctx - 1)
+
     def send_own_kv(h):
-        @pl.when(jnp.logical_not(last_dev))
+        @pl.when(not_last)
         def _():
             kv_copy(0, 0, h, cols(k_hbm, h)).start()
             kv_copy(0, 1, h, cols(v_hbm, h)).start()
 
     def send_own_qo(a, h):
-        @pl.when(jnp.logical_not(first_dev))
+        @pl.when(not_first)
         def _():
             qo_copy(0, a, h, cols(q_hbm, h) if a == 0 else own_do.at[h]).start()
 
     def relay_kv(h):
         for a in range(2):
-            @pl.when(jnp.logical_not(first_dev))
+            @pl.when(not_first)
             def _():
                 arrived(kv, kv_recv, 0, a, h)
 
-            @pl.when((me > 0) & (me < n_ctx - 1))
+            @pl.when(inner)
             def _():
                 kv_copy(1, a, h).start()
-
-            @pl.when(last_dev)
-            def _():
-                arrived(kv, kv_recv, 2, a, h)
-                kv_copy(0, a, h, kv.at[2, a, h]).start()
 
     def wait_far_kv(h):
         for a in range(2):
@@ -144,30 +155,24 @@
             def _():
                 arrived(kv, kv_recv, 1, a, h)
 
-            @pl.when(last_dev)
-            def _():
-                arrived(kv, kv_recv, 3, a, h)
-                kv_copy(1, a, h, kv.at[3, a, h]).start()
+    def forward_keys(hop, h):
+        @pl.when(last_dev)
+        def _():
+            arrived(kv, kv_recv, hop + 2, 0, h)
+            kv_copy(hop, 0, h, kv.at[hop + 2, 0, h]).start()
+
+    def forward_queries(hop, h):
+        @pl.when(first_dev)
+        def _():
+            arrived(qo, qo_recv, hop + 2, 0, h)
+            qo_copy(hop, 0, h, qo.at[hop + 2, 0, h]).start()
 
     def relay_qo(a, h):
-        @pl.when(jnp.logical_not(last_dev))
-        def _():
-            arrived(qo, qo_recv, 0, a, h)
-
-        @pl.when((me > 0) & (me < n_ctx - 1))
+        arrived(qo, qo_recv, 0, a, h)
+
+        @pl.when(me > 0)
         def _():
             qo_copy(1, a, h).start()
-
-        @pl.when(first_dev)
-        def _():
-            arrived(qo, qo_recv, 2, a, h)
-            qo_copy(0, a, h, qo.at[2, a, h]).start()
-
-    def forward_far_qo(a, h):
-        @pl.when(first_dev)
-        def _():
-            arrived(qo, qo_recv, 3, a, h)
-            qo_copy(1, a, h, qo.at[3, a, h]).start()
 
     def wait_far_qo(h):
         for a in range(2):
@@ -175,11 +180,16 @@
             def _():
                 arrived(qo, qo_recv, 1, a, h)
 
+    def relay_do(h):
+        @pl.when(not_last)
+        def _():
+            relay_qo(1, h)
+
     cot_core = remote(c_hbm, cot.at[1], cot_send.at[0], cot_recv.at[0], (me, core_mate))
     cot_x = remote(c_hbm, cot.at[2], cot_send.at[1], cot_recv.at[1], (me, x_mate))
     cot_relay = remote(cot.at[2], cot.at[3], cot_send.at[2], cot_recv.at[2], (me, core_mate))
 
-    pl.semaphore_wait(barrier, 6)
+    pl.semaphore_wait(barrier, 6 + at_end + at_start)
     cot_x.start()
     cot_core.start()
     for h in range(heads):
@@ -226,18 +236,25 @@
     grad = dot_nt(cot[0], w_block(grp))
     cot_core.wait_recv()
     grad += dot_nt(cot[1], w_block(core_mate))
-    for h in range(heads):
-        relay_qo(0, h)
-    relay_kv(0)
+
+    @pl.when(not_last & jnp.logical_not(end_dev))
+    def _():
+        for h in range(heads):
+            relay_qo(0, h)
+
     cot_x.wait_recv()
     cot_relay.start()
     grad += dot_nt(cot[2], w_block(x_mate))
-    relay_kv(1)
     cot_relay.wait_recv()
     grad += dot_nt(cot[3], w_block(x_core_mate))
     for h in range(heads):
         own_do[h] = grad[:, h * HD : (h + 1) * HD].astype(BF16)
         send_own_qo(1, h)
+    for h in range(heads):
+        forward_queries(0, h)
+    for h in range(3):
+        relay_kv(h)
+        forward_keys(0, h)
     for copy in head_loads:
         copy.wait()
 
@@ -295,26 +312,32 @@
         out_ref[2, :, h * HD : (h + 1) * HD] = grad_k.astype(BF16)
         out_ref[3, :, h * HD : (h + 1) * HD] = grad_v.astype(BF16)
 
-    relay_kv(2)
-    for h in range(heads):
-        forward_far_qo(0, h)
+    for h in range(heads):
+        forward_queries(1, h)
+
     relay_kv(3)
+    forward_keys(0, 3)
+
+    @pl.when(end_dev)
+    def _():
+        for h in range(heads):
+            relay_qo(0, h)
+
+    for h in range(3):
+        forward_keys(1, h)
     wait_far_kv(0)
     query_side(0)
-    relay_qo(1, 0)
-    relay_qo(1, 1)
+    relay_do(0)
+    relay_do(1)
+    forward_keys(1, 3)
     wait_far_kv(1)
-    forward_far_qo(1, 0)
     query_side(1)
-    relay_qo(1, 2)
-    relay_qo(1, 3)
+    relay_do(2)
+    relay_do(3)
     wait_far_kv(2)
-    forward_far_qo(1, 1)
     query_side(2)
     wait_far_kv(3)
-    forward_far_qo(1, 2)
     query_side(3)
-    forward_far_qo(1, 3)
 
     stat_copies = [
         remote(stats, stats_in.at[d], st_send.at[d], st_recv.at[d], (target, grp))
@@ -350,18 +373,25 @@
     cot_core.wait_send()
     cot_x.wait_send()
     cot_relay.wait_send()
-    for a in range(2):
-        for h in range(heads):
-            kv_copy(0, a, h).wait_send()
-            qo_copy(0, a, h).wait_send()
-
-            @pl.when(jnp.logical_not(first_dev))
-            def _():
-                kv_copy(1, a, h).wait_send()
-
-            @pl.when(jnp.logical_not(last_dev))
-            def _():
-                qo_copy(1, a, h).wait_send()
+    for h in range(heads):
+        kv_copy(0, 0, h).wait_send()
+        qo_copy(0, 0, h).wait_send()
+
+        @pl.when(not_last)
+        def _():
+            kv_copy(0, 1, h).wait_send()
+            qo_copy(1, 0, h).wait_send()
+
+        @pl.when(not_first)
+        def _():
+            qo_copy(0, 1, h).wait_send()
+            kv_copy(1, 0, h).wait_send()
+
+        @pl.when(inner)
+        def _():
+            kv_copy(1, 1, h).wait_send()
+            qo_copy(1, 1, h).wait_send()
+
     for copy in stat_copies + [mix_a, mix_c, mix_x]:
         copy.wait_send()
 
@@ -428,7 +458,7 @@
     return pl.pallas_call(
         spread,
         out_shape=(tile,) * 4,
-        in_specs=[any_spec],
+        in_specs=[vmem_spec],
         out_specs=(any_spec,) * 4,
         scratch_shapes=[dma((4,))],
     )(four)

time: 132 us -> 77.3 us (0.59)
  the two profiles are of different devices: /device:TPU:1 before, /device:TPU:6 now
where the time goes in v3:
time: 77.3 us; the launch traced here: 76 us
  Pallas kernels  74 us (96%)
  local copies, waits for them, and re-layouts  1.31 us (2%)
    pallas_call x1, Pallas kernels, per_device(): pl.pallas_call(functools.partial(kernel, n_ctx, groups), out_shape=jax.Sh...  71.4 us
    pallas_call x1, Pallas kernels, per_device(): pl.pallas_call(spread, out_shape=(tile,) * 4, in_specs=[vmem_spec], out_s...  2.58 us

profile of v3, /device:TPU:6, one launch (start us, length us, event | category | flops | bytes accessed | tf_op | source)
XLA Modules:
  0.0 76.0 jit_solution(6337934585425498973)
XLA Ops:
  0.6 1.3 %pad_bitcast_fusion.offs = s32[24,128]{1,0:T(8,128)} fusion(s32[2056]{0:T(1024)} %param.11), kind=kLoop, calls=%fused_computation | loop fusion | bytes 20512 | tf_op jit(solution)/shard_map/reshape | solution.py:417
  1.9 71.4 %shard_map.93.all_ref = bf16[4,384,512]{2,1,0:T(8,128)(2,1)} custom-call(bf16[384,512]{1,0:T(8,128)(2,1)} %q_hbm.1, bf16[384,512]{1,0:T(8,128)(2,1)} %k_hbm.1, bf16[384,512]{1,0:T(8,128)(2,1)} %v_hbm.1, bf16[512,2048]{1,0:T(8,128)(2,1)} %w_hbm.1, bf16[384,512]{1,0:T(8,128)(2,1)} %c_hbm.1, s32[24,128]{1,0:T(8,128)} %pad_bitcast_fusion.offs), custom_call_target="tpu_custom_call" | custom-call | tf_op jit(solution)/shard_map/pallas_call | solution.py:422
  73.4 2.6 %shard_map.94 = (bf16[384,512]{1,0:T(8,128)(2,1)}, bf16[384,512]{1,0:T(8,128)(2,1)}, bf16[384,512]{1,0:T(8,128)(2,1)}, bf16[384,512]{1,0:T(8,128)(2,1)}) custom-call(bf16[4,384,512]{2,1,0:T(8,128)(2,1)} %shard_map.93.all_ref), custom_call_target="tpu_custom_call" | custom-call | tf_op jit(solution)/shard_map/pallas_call | solution.py:458

commit v4 on v3

v4 whole, which is shorter than its diff:
```python
import functools
import math

import jax
import jax.numpy as jnp
from jax import lax
from jax.experimental import pallas as pl
from jax.experimental.pallas import tpu as pltpu
from jax.sharding import PartitionSpec as P

HD = 128
BLOCK = 128
PREV = 3
NEG_FILL = -1e30
LOG2E = math.log2(math.e)
F32 = jnp.float32
BF16 = jnp.bfloat16
MESH = pl.DeviceIdType.MESH


def dot_nn(a, b):
    return lax.dot_general(a, b, (((1,), (0,)), ((), ())), preferred_element_type=F32)


def dot_nt(a, b):
    return lax.dot_general(a, b, (((1,), (1,)), ((), ())), preferred_element_type=F32)


def dot_tn(a, b):
    return lax.dot_general(a, b, (((0,), (0,)), ((), ())), preferred_element_type=F32)


def kernel(
    n_ctx, groups, q_hbm, k_hbm, v_hbm, w_hbm, c_hbm, offs,
    out_ref,
    own_q, own_k, own_v, own_do, w_ref, cot, kv, qo, stats, stats_in,
    att, acc, mix_out, mix_in,
    load_sem, cot_send, cot_recv, kv_send, kv_recv, qo_send, qo_recv,
    st_send, st_recv, mix_send, mix_recv, seam_sem,
):
    rows = q_hbm.shape[0]
    feats = q_hbm.shape[1]
    heads = feats // HD
    scale = 1.0 / math.sqrt(HD)
    scale2 = scale * LOG2E
    blocks = rows // BLOCK
    last = blocks - 1
    half = n_ctx // 2
    me = lax.axis_index("ctx")
    grp = lax.axis_index("head")
    first_dev = me == 0
    last_dev = me == n_ctx - 1
    end_dev = me == half - 1
    start_dev = me == half
    at_end = end_dev.astype(jnp.int32)
    at_start = start_dev.astype(jnp.int32)
    is_last = last_dev.astype(jnp.int32)
    is_first = first_dev.astype(jnp.int32)
    key_right = me + 1 + at_end * (n_ctx - 1 - half) + is_last * (half - n_ctx)
    query_left = me - 1 + at_start * (1 - half) + is_first * half
    before_end = me == half - 2
    after_start = me == half + 1
    core = lax.rem(grp, 2)
    pair = grp // 2
    core_mate = pair * 2 + (1 - core)
    x_mate = (1 - pair) * 2 + core
    x_core_mate = (1 - pair) * 2 + (1 - core)

    barrier = pltpu.get_barrier_semaphore()
    def greet(target, sem=barrier):
        pl.semaphore_signal(sem, inc=1, device_id=target, device_id_type=MESH)

    greet((me, core_mate))
    greet((me, x_mate))
    greetings = (
        (me > 0, me - 1),
        ((me < n_ctx - 1) & (me != half - 1), me + 1),
        ((me < n_ctx - 2) & (me != half - 1) & (me != half - 2), me + 2),
        (last_dev, half - 1),
        (start_dev, n_ctx - 1),
        (first_dev, half),
        (first_dev, half - 1),
        (start_dev, half - 2),
        (after_start, half - 1),
    )
    for condition, target in greetings:
        @pl.when(condition)
        def _():
            greet((target, grp))

    def as_int(condition):
        return condition.astype(jnp.int32)

    greeted = (
        2
        + as_int(me < n_ctx - 1)
        + as_int((me > 0) & (me != half))
        + as_int((me > 1) & (me != half) & (me != half + 1))
        + 3 * at_end + is_last + at_start + as_int(before_end)
    )

    def part_rows(b):
        return slice(b * BLOCK, (b + 1) * BLOCK)

    pairs = (
        (c_hbm, cot.at[0]), (w_hbm, w_ref), (q_hbm, own_q), (k_hbm, own_k), (v_hbm, own_v),
    )
    loads = [
        pltpu.make_async_copy(src, dst, load_sem.at[i]) for i, (src, dst) in enumerate(pairs)
    ]
    for copy in loads:
        copy.start()

    def remote(src, dst, send, recv, target):
        return pltpu.make_async_remote_copy(
            src_ref=src, dst_ref=dst, send_sem=send, recv_sem=recv,
            device_id=target, device_id_type=MESH,
        )

    def kv_copy(hop, a, b, src=None):
        slot = hop + 2 * at_end if a == 0 else hop
        return remote(
            kv.at[0, a, part_rows(b)] if src is None else src, kv.at[slot, a, part_rows(b)],
            kv_send.at[hop, a, b], kv_recv.at[slot, a, b],
            (key_right if a == 0 else me + 1, grp),
        )

    def qo_copy(hop, a, b, src=None):
        slot = hop + 2 * at_start if a == 0 else hop
        return remote(
            qo.at[0, a, part_rows(b)] if src is None else src, qo.at[slot, a, part_rows(b)],
            qo_send.at[hop, a, b], qo_recv.at[slot, a, b],
            (query_left if a == 0 else me - 1, grp),
        )

    def arrived(buf, sems, slot, a, b):
        part, sem = buf.at[slot, a, part_rows(b)], sems.at[slot, a, b]
        remote(part, part, sem, sem, (me, core_mate)).wait_recv()

    not_first = jnp.logical_not(first_dev)
    not_last = jnp.logical_not(last_dev)
    inner = (me > 0) & (me < n_ctx - 1)

    def send_own_kv(b):
        @pl.when(not_last)
        def _():
            kv_copy(0, 0, b, k_hbm.at[part_rows(b)]).start()
            kv_copy(0, 1, b, v_hbm.at[part_rows(b)]).start()

    def send_own_qo(a, b):
        @pl.when(not_first)
        def _():
            qo_copy(0, a, b, (q_hbm if a == 0 else own_do).at[part_rows(b)]).start()

    def relay_kv(b):
        for a in range(2):
            @pl.when(not_first)
            def _():
                arrived(kv, kv_recv, 0, a, b)

            @pl.when(inner)
            def _():
                kv_copy(1, a, b).start()

    def wait_far_kv(b):
        for a in range(2):
            @pl.when(me > 1)
            def _():
                arrived(kv, kv_recv, 1, a, b)

    def forward_keys(hop, b):
        @pl.when(last_dev)
        def _():
            arrived(kv, kv_recv, hop + 2, 0, b)
            kv_copy(hop, 0, b, kv.at[hop + 2, 0, part_rows(b)]).start()

    def forward_queries(hop, b):
        @pl.when(first_dev)
        def _():
            arrived(qo, qo_recv, hop + 2, 0, b)
            qo_copy(hop, 0, b, qo.at[hop + 2, 0, part_rows(b)]).start()

    def relay_qo(a, b):
        arrived(qo, qo_recv, 0, a, b)

        @pl.when(me > 0)
        def _():
            qo_copy(1, a, b).start()

    def wait_far_qo(b):
        for a in range(2):
            @pl.when(me < n_ctx - 2)
            def _():
                arrived(qo, qo_recv, 1, a, b)

    def relay_do(b):
        @pl.when(not_last & jnp.logical_not(start_dev))
        def _():
            relay_qo(1, b)

    cot_core = remote(c_hbm, cot.at[1], cot_send.at[0], cot_recv.at[0], (me, core_mate))
    cot_x = remote(c_hbm, cot.at[2], cot_send.at[1], cot_recv.at[1], (me, x_mate))
    cot_relay = remote(cot.at[2], cot.at[3], cot_send.at[2], cot_recv.at[2], (me, core_mate))

    pl.semaphore_wait(barrier, greeted)

    @pl.when(end_dev)
    def _():
        for target in (half, half + 1, 0):
            greet((target, grp), seam_sem)

    @pl.when(before_end)
    def _():
        greet((half, grp), seam_sem)

    cot_x.start()
    cot_core.start()
    order = range(last, -1, -1)
    late_queries = end_dev | before_end
    for b in order:
        @pl.when(jnp.logical_not(end_dev))
        def _():
            send_own_qo(0, b)

        send_own_kv(b)

    @pl.when(first_dev)
    def _():
        kv[0] = jnp.zeros(kv.shape[1:], BF16)

    @pl.when(me <= 1)
    def _():
        kv[1] = jnp.zeros(kv.shape[1:], BF16)

    @pl.when(last_dev)
    def _():
        qo[0] = jnp.zeros(qo.shape[1:], BF16)
        stats_in[0] = jnp.zeros(stats_in.shape[1:], F32)

    @pl.when(me >= n_ctx - 2)
    def _():
        qo[1] = jnp.zeros(qo.shape[1:], BF16)
        stats_in[1] = jnp.zeros(stats_in.shape[1:], F32)

    base = me * rows
    q_pos = base + lax.broadcasted_iota(jnp.int32, (rows, 128), 0)
    first = jnp.zeros((rows, 128), jnp.int32)
    lists = offs[...]
    turned = pltpu.roll(lists, 128 - PREV, 1)
    lane = lax.broadcasted_iota(jnp.int32, lists.shape, 1)
    ahead = jnp.where(lane < 128 - PREV, turned, pltpu.roll(turned, lists.shape[0] - 1, 0))
    for g in range(groups):
        starts = jnp.broadcast_to(lists[g : g + 1, :], (rows, 128))
        later = jnp.broadcast_to(ahead[g : g + 1, :], (rows, 128))
        first = jnp.maximum(first, jnp.where(later <= q_pos, starts, 0))
    first = (first - base).astype(F32)
    low = jnp.max(first.T, axis=0, keepdims=True)
    stats[...] = jnp.zeros(stats.shape, F32)
    for b in order:
        stats[b, 2 * heads : 2 * heads + 1, :] = low[:, part_rows(b)]

    def w_block(index):
        return w_ref[:, pl.ds(pl.multiple_of(index * feats, feats), feats)]

    loads[0].wait()
    loads[1].wait()
    grad = dot_nt(cot[0], w_block(grp))
    cot_core.wait_recv()
    grad += dot_nt(cot[1], w_block(core_mate))

    @pl.when(not_last & jnp.logical_not(late_queries))
    def _():
        for b in order:
            relay_qo(0, b)

    @pl.when(jnp.logical_not(start_dev))
    def _():
        relay_kv(last)

    cot_x.wait_recv()
    cot_relay.start()
    grad += dot_nt(cot[2], w_block(x_mate))
    for b in order[:-1]:
        forward_keys(0, b)

    @pl.when(jnp.logical_not(start_dev))
    def _():
        for b in order[1:-1]:
            relay_kv(b)

    @pl.when(end_dev)
    def _():
        for b in order:
            send_own_qo(0, b)

    cot_relay.wait_recv()
    grad += dot_nt(cot[3], w_block(x_core_mate))
    own_do[...] = grad.astype(BF16)

    @pl.when(start_dev)
    def _():
        pl.semaphore_wait(seam_sem, 2)

    @pl.when(first_dev)
    def _():
        pl.semaphore_wait(seam_sem, 1)

    @pl.when(after_start)
    def _():
        pl.semaphore_wait(seam_sem, 1)

    for b in order:
        send_own_qo(1, b)

    @pl.when(start_dev)
    def _():
        for b in order:
            relay_qo(1, b)

    for b in order:
        forward_queries(0, b)
    for copy in loads[2:]:
        copy.wait()

    def head_cols(h):
        return slice(h * HD, (h + 1) * HD)

    def query_side(b):
        part = part_rows(b)
        floor = low[:, part]
        for h in range(heads):
            col = head_cols(h)
            query = own_q[part, col]
            grad_o = own_do[part, col]
            own_rows = slice(0, (b + 1) * BLOCK)
            far_rows = slice(b * BLOCK, rows)
            key_tiles = (own_k[own_rows, col], kv[0, 0, :, col], kv[1, 0, far_rows, col])
            value_tiles = (own_v[own_rows, col], kv[0, 1, :, col], kv[1, 1, far_rows, col])
            scores = []
            for d in range(3):
                shape = (key_tiles[d].shape[0], BLOCK)
                start = b * BLOCK if d == 2 else 0
                key_row = lax.broadcasted_iota(jnp.int32, shape, 0).astype(F32)
                mask = key_row >= floor + float(d * rows - start)
                if d == 0:
                    query_col = lax.broadcasted_iota(jnp.int32, shape, 1).astype(F32)
                    mask = mask & (key_row <= query_col + float(b * BLOCK))
                raw = dot_nt(key_tiles[d], query) * scale2
                scores.append(jnp.where(mask, raw, NEG_FILL))
            top = functools.reduce(
                jnp.maximum, [jnp.max(s, axis=0, keepdims=True) for s in scores]
            )
            expd = [jnp.exp2(s - top) for s in scores]
            total = functools.reduce(jnp.add, [jnp.sum(e, axis=0, keepdims=True) for e in expd])
            inverse = 1.0 / total
            probs = [e * inverse for e in expd]
            probs_b = [p.astype(BF16) for p in probs]
            mixed_t = sum(dot_tn(value_tiles[d], probs_b[d]) for d in range(3))
            attended = mixed_t.T.astype(BF16)
            att[part, col] = attended
            product = grad_o.astype(F32) * attended.astype(F32)
            delta = jnp.sum(product.T, axis=0, keepdims=True)
            stats[b, h : h + 1, :] = top + jnp.log2(total)
            stats[b, heads + h : heads + h + 1, :] = delta
            grads_b = []
            for d in range(3):
                grad_p = dot_nt(value_tiles[d], grad_o)
                grads_b.append((scale * probs[d] * (grad_p - delta)).astype(BF16))
            dq_t = sum(dot_tn(key_tiles[d], grads_b[d]) for d in range(3))
            out_ref[1, part, col] = dq_t.T.astype(BF16)
            grad_k = dot_nn(grads_b[0], query)
            grad_v = dot_nn(probs_b[0], grad_o)
            if b == last:
                acc[0, :, col] = grad_k
                acc[1, :, col] = grad_v
            else:
                acc[0, own_rows, col] += grad_k
                acc[1, own_rows, col] += grad_v

    def key_side(b):
        part = part_rows(b)
        for h in range(heads):
            col = head_cols(h)
            for d in range(2):
                start = b * BLOCK if d == 1 else 0
                near = slice(start, rows)
                query = qo[d, 0, part, col]
                grad_o = qo[d, 1, part, col]
                key_row = lax.broadcasted_iota(jnp.int32, (rows - start, BLOCK), 0).astype(F32)
                floor = stats_in[d, b, 2 * heads : 2 * heads + 1, :]
                floor = floor + float((d + 1) * rows - start)
                log_total = stats_in[d, b, h : h + 1, :]
                delta = stats_in[d, b, heads + h : heads + h + 1, :]
                raw = dot_nt(own_k[near, col], query) * scale2
                probs = jnp.where(key_row >= floor, jnp.exp2(raw - log_total), 0.0)
                acc[1, near, col] += dot_nn(probs.astype(BF16), grad_o)
                grad_p = dot_nt(own_v[near, col], grad_o)
                grad_s = (scale * probs * (grad_p - delta)).astype(BF16)
                acc[0, near, col] += dot_nn(grad_s, query)

    def stat_copy(b, d):
        return remote(
            stats.at[b], stats_in.at[d, b], st_send.at[d, b], st_recv.at[d, b], (me - 1 - d, grp)
        )

    def send_stats(b):
        for d in range(2):
            @pl.when(me > d)
            def _():
                stat_copy(b, d).start()

    def wait_queries(b):
        wait_far_qo(b)
        for d in range(2):
            @pl.when(me < n_ctx - 1 - d)
            def _():
                stat_copy(b, d).wait_recv()

    def mix_copy(i, b):
        part = part_rows(b)
        return remote(
            mix_out.at[i, part], mix_in.at[i, part], mix_send.at[i, b], mix_recv.at[i, b],
            (me, x_mate if i == 2 else core_mate),
        )

    def mix_near(b):
        part = part_rows(b)
        for i, owner in enumerate((x_core_mate, core_mate)):
            mix_out[i, part] = dot_nn(att[part], w_block(owner)).astype(BF16)
            mix_copy(i, b).start()

    def mix_far(b):
        part = part_rows(b)
        far_part = dot_nn(att[part], w_block(x_mate))
        mix_copy(0, b).wait_recv()
        mix_out[2, part] = (far_part + mix_in[0, part].astype(F32)).astype(BF16)
        mix_copy(2, b).start()

    def mix_finish(b):
        part = part_rows(b)
        own_part = dot_nn(att[part], w_block(grp))
        mix_copy(1, b).wait_recv()
        own_part += mix_in[1, part].astype(F32)
        mix_copy(2, b).wait_recv()
        out_ref[0, part] = (own_part + mix_in[2, part].astype(F32)).astype(BF16)

    @pl.when(start_dev)
    def _():
        for b in order[:-1]:
            relay_kv(b)

    for b in order:
        forward_queries(1, b)
    relay_kv(0)
    forward_keys(0, 0)

    @pl.when(late_queries)
    def _():
        for b in order:
            relay_qo(0, b)

    for b in order[:-1]:
        forward_keys(1, b)
    relay_do(last)
    for b in order:
        wait_far_kv(b)
        if b == last:
            forward_keys(1, 0)
        query_side(b)
        send_stats(b)
        mix_near(b)
        if b == last:
            for later in order[1:]:
                relay_do(later)
        elif b > 0:
            wait_queries(b + 1)
            key_side(b + 1)
        mix_far(b)
    wait_queries(1)
    key_side(1)
    wait_queries(0)
    key_side(0)
    out_ref[2] = acc[0].astype(BF16)
    out_ref[3] = acc[1].astype(BF16)
    for b in order:
        mix_finish(b)

    cot_core.wait_send()
    cot_x.wait_send()
    cot_relay.wait_send()
    for b in order:
        kv_copy(0, 0, b).wait_send()
        qo_copy(0, 0, b).wait_send()

        @pl.when(not_last)
        def _():
            kv_copy(0, 1, b).wait_send()
            qo_copy(1, 0, b).wait_send()

        @pl.when(not_first)
        def _():
            qo_copy(0, 1, b).wait_send()
            kv_copy(1, 0, b).wait_send()

        @pl.when(inner)
        def _():
            kv_copy(1, 1, b).wait_send()
            qo_copy(1, 1, b).wait_send()

    for b in order:
        for d in range(2):
            @pl.when(me > d)
            def _():
                stat_copy(b, d).wait_send()
        for i in range(3):
            mix_copy(i, b).wait_send()


def spread(all_ref, *refs):
    outs, sems = refs[:-1], refs[-1]
    copies = [
        pltpu.make_async_copy(all_ref.at[i], out, sems.at[i]) for i, out in enumerate(outs)
    ]
    for copy in copies:
        copy.start()
    for copy in copies:
        copy.wait()


def per_device(n_ctx, queries, key_rows, value_rows, out_weight, cotangent, offsets):
    rows, feats = queries.shape
    blocks = rows // BLOCK
    count = offsets.shape[0]
    groups = -(-count // 128)
    padded = -(-(groups + 1) // 8) * 8
    offs = jnp.pad(offsets, (0, padded * 128 - count), constant_values=2**30)
    offs = offs.reshape(padded, 128)
    any_spec = pl.BlockSpec(memory_space=pl.ANY)
    vmem_spec = pl.BlockSpec(memory_space=pltpu.VMEM)
    tile = jax.ShapeDtypeStruct((rows, feats), BF16)
    dma = pltpu.SemaphoreType.DMA
    four = pl.pallas_call(
        functools.partial(kernel, n_ctx, groups),
        out_shape=jax.ShapeDtypeStruct((4, rows, feats), BF16),
        in_specs=[any_spec] * 5 + [vmem_spec],
        out_specs=vmem_spec,
        scratch_shapes=[
            pltpu.VMEM((rows, feats), BF16),
            pltpu.VMEM((rows, feats), BF16),
            pltpu.VMEM((rows, feats), BF16),
            pltpu.VMEM((rows, feats), BF16),
            pltpu.VMEM(out_weight.shape, BF16),
            pltpu.VMEM((4, rows, feats), BF16),
            pltpu.VMEM((4, 2, rows, feats), BF16),
            pltpu.VMEM((4, 2, rows, feats), BF16),
            pltpu.VMEM((blocks, 16, BLOCK), F32),
            pltpu.VMEM((2, blocks, 16, BLOCK), F32),
            pltpu.VMEM((rows, feats), BF16),
            pltpu.VMEM((2, rows, feats), F32),
            pltpu.VMEM((3, rows, feats), BF16),
            pltpu.VMEM((3, rows, feats), BF16),
            dma((5,)),
            dma((3,)),
            dma((3,)),
            dma((2, 2, blocks)),
            dma((4, 2, blocks)),
            dma((2, 2, blocks)),
            dma((4, 2, blocks)),
            dma((2, blocks)),
            dma((2, blocks)),
            dma((3, blocks)),
            dma((3, blocks)),
            pltpu.SemaphoreType.REGULAR,
        ],
        compiler_params=pltpu.CompilerParams(
            collective_id=0, has_side_effects=True, vmem_limit_bytes=58 * 1024 * 1024
        ),
    )(queries, key_rows, value_rows, out_weight, cotangent, offs)
    return pl.pallas_call(
        spread,
        out_shape=(tile,) * 4,
        in_specs=[vmem_spec],
        out_specs=(any_spec,) * 4,
        scratch_shapes=[dma((4,))],
    )(four)


def solution(mesh):
    in_specs = (
        P("ctx", "head"),
        P("ctx", "head"),
        P("ctx", "head"),
        P("head", None),
        P("ctx", "head"),
        P(),
    )
    out_specs = (P("ctx", "head"), P("ctx", "head"), P("ctx", "head"), P("ctx", "head"))
    return jax.shard_map(
        functools.partial(per_device, mesh.shape["ctx"]),
        mesh=mesh,
        in_specs=in_specs,
        out_specs=out_specs,
        check_vma=False,
    )
```

time: 77.3 us -> 75.4 us (0.975); the launches traced: 76 us -> 75.2 us
  Pallas kernels: 74 us -> 73.2 us
where the time goes in v4:
time: 75.4 us; the launch traced here: 75.2 us
  Pallas kernels  73.2 us (97%)
  local copies, waits for them, and re-layouts  1.31 us (2%)
    pallas_call x1, Pallas kernels, per_device(): pl.pallas_call(functools.partial(kernel, n_ctx, groups), out_shape=jax.Sh...  70.7 us
    pallas_call x1, Pallas kernels, per_device(): pl.pallas_call(spread, out_shape=(tile,) * 4, in_specs=[vmem_spec], out_s...  2.58 us

profile of v4, /device:TPU:6, one launch (start us, length us, event | category | flops | bytes accessed | tf_op | source)
XLA Modules:
  0.0 75.2 jit_solution(18043351945261561397)
XLA Ops:
  0.6 1.3 %pad_bitcast_fusion.offs = s32[24,128]{1,0:T(8,128)} fusion(s32[2056]{0:T(1024)} %param.11), kind=kLoop, calls=%fused_computation | loop fusion | bytes 20512 | tf_op jit(solution)/shard_map/reshape | solution.py:537
  1.9 70.7 %shard_map.93.all_ref = bf16[4,384,512]{2,1,0:T(8,128)(2,1)} custom-call(bf16[384,512]{1,0:T(8,128)(2,1)} %q_hbm.1, bf16[384,512]{1,0:T(8,128)(2,1)} %k_hbm.1, bf16[384,512]{1,0:T(8,128)(2,1)} %v_hbm.1, bf16[512,2048]{1,0:T(8,128)(2,1)} %w_hbm.1, bf16[384,512]{1,0:T(8,128)(2,1)} %c_hbm.1, s32[24,128]{1,0:T(8,128)} %pad_bitcast_fusion.offs), custom_call_target="tpu_custom_call" | custom-call | tf_op jit(solution)/shard_map/pallas_call | solution.py:542
  72.6 2.6 %shard_map.94 = (bf16[384,512]{1,0:T(8,128)(2,1)}, bf16[384,512]{1,0:T(8,128)(2,1)}, bf16[384,512]{1,0:T(8,128)(2,1)}, bf16[384,512]{1,0:T(8,128)(2,1)}) custom-call(bf16[4,384,512]{2,1,0:T(8,128)(2,1)} %shard_map.93.all_ref), custom_call_target="tpu_custom_call" | custom-call | tf_op jit(solution)/shard_map/pallas_call | solution.py:579

commit v5 on v4

--- a/solution.py
+++ b/solution.py
@@ -288,11 +288,6 @@
         for b in order[1:-1]:
             relay_kv(b)
 
-    @pl.when(end_dev)
-    def _():
-        for b in order:
-            send_own_qo(0, b)
-
     cot_relay.wait_recv()
     grad += dot_nt(cot[3], w_block(x_core_mate))
     own_do[...] = grad.astype(BF16)
@@ -309,12 +304,22 @@
     def _():
         pl.semaphore_wait(seam_sem, 1)
 
+    @pl.when(end_dev)
+    def _():
+        relay_kv(0)
+
     for b in order:
         send_own_qo(1, b)
 
+    @pl.when(end_dev)
+    def _():
+        for b in order:
+            send_own_qo(0, b)
+
     @pl.when(start_dev)
     def _():
         for b in order:
+            relay_kv(b)
             relay_qo(1, b)
 
     for b in order:
@@ -444,21 +449,14 @@
         mix_copy(2, b).wait_recv()
         out_ref[0, part] = (own_part + mix_in[2, part].astype(F32)).astype(BF16)
 
-    @pl.when(start_dev)
-    def _():
-        for b in order[:-1]:
-            relay_kv(b)
-
     for b in order:
         forward_queries(1, b)
-    relay_kv(0)
+
+    @pl.when(jnp.logical_not(end_dev | start_dev))
+    def _():
+        relay_kv(0)
+
     forward_keys(0, 0)
-
-    @pl.when(late_queries)
-    def _():
-        for b in order:
-            relay_qo(0, b)
-
     for b in order[:-1]:
         forward_keys(1, b)
     relay_do(last)
@@ -470,6 +468,11 @@
         send_stats(b)
         mix_near(b)
         if b == last:
+            @pl.when(late_queries)
+            def _():
+                for late in order:
+                    relay_qo(0, late)
+
             for later in order[1:]:
                 relay_do(later)
         elif b > 0:

time: 75.4 us -> 75.4 us (level)
  no operation moved by 1% of the time
where the time goes in v5:
time: 75.4 us; the launch traced here: 75.2 us
  Pallas kernels  73.2 us (97%)
  local copies, waits for them, and re-layouts  1.31 us (2%)
    pallas_call x1, Pallas kernels, per_device(): pl.pallas_call(functools.partial(kernel, n_ctx, groups), out_shape=jax.Sh...  70.7 us
    pallas_call x1, Pallas kernels, per_device(): pl.pallas_call(spread, out_shape=(tile,) * 4, in_specs=[vmem_spec], out_s...  2.58 us

profile of v5, /device:TPU:6, one launch (start us, length us, event | category | flops | bytes accessed | tf_op | source)
XLA Modules:
  0.0 75.2 jit_solution(9903508657617844264)
XLA Ops:
  0.6 1.3 %pad_bitcast_fusion.offs = s32[24,128]{1,0:T(8,128)} fusion(s32[2056]{0:T(1024)} %param.11), kind=kLoop, calls=%fused_computation | loop fusion | bytes 20512 | tf_op jit(solution)/shard_map/reshape | solution.py:540
  1.9 70.7 %shard_map.93.all_ref = bf16[4,384,512]{2,1,0:T(8,128)(2,1)} custom-call(bf16[384,512]{1,0:T(8,128)(2,1)} %q_hbm.1, bf16[384,512]{1,0:T(8,128)(2,1)} %k_hbm.1, bf16[384,512]{1,0:T(8,128)(2,1)} %v_hbm.1, bf16[512,2048]{1,0:T(8,128)(2,1)} %w_hbm.1, bf16[384,512]{1,0:T(8,128)(2,1)} %c_hbm.1, s32[24,128]{1,0:T(8,128)} %pad_bitcast_fusion.offs), custom_call_target="tpu_custom_call" | custom-call | tf_op jit(solution)/shard_map/pallas_call | solution.py:545
  72.6 2.6 %shard_map.94 = (bf16[384,512]{1,0:T(8,128)(2,1)}, bf16[384,512]{1,0:T(8,128)(2,1)}, bf16[384,512]{1,0:T(8,128)(2,1)}, bf16[384,512]{1,0:T(8,128)(2,1)}) custom-call(bf16[4,384,512]{2,1,0:T(8,128)(2,1)} %shard_map.93.all_ref), custom_call_target="tpu_custom_call" | custom-call | tf_op jit(solution)/shard_map/pallas_call | solution.py:582

commit v6 on v5

--- a/solution.py
+++ b/solution.py
@@ -118,11 +118,12 @@
         )
 
     def kv_copy(hop, a, b, src=None):
-        slot = hop + 2 * at_end if a == 0 else hop
+        by_last = a == 0 and hop == 0
+        slot = hop + 2 * at_end if by_last else hop
         return remote(
             kv.at[0, a, part_rows(b)] if src is None else src, kv.at[slot, a, part_rows(b)],
             kv_send.at[hop, a, b], kv_recv.at[slot, a, b],
-            (key_right if a == 0 else me + 1, grp),
+            (key_right if by_last else me + 1, grp),
         )
 
     def qo_copy(hop, a, b, src=None):
@@ -457,13 +458,9 @@
         relay_kv(0)
 
     forward_keys(0, 0)
-    for b in order[:-1]:
-        forward_keys(1, b)
     relay_do(last)
     for b in order:
         wait_far_kv(b)
-        if b == last:
-            forward_keys(1, 0)
         query_side(b)
         send_stats(b)
         mix_near(b)
@@ -503,10 +500,10 @@
         @pl.when(not_first)
         def _():
             qo_copy(0, 1, b).wait_send()
+
+        @pl.when(inner)
+        def _():
             kv_copy(1, 0, b).wait_send()
-
-        @pl.when(inner)
-        def _():
             kv_copy(1, 1, b).wait_send()
             qo_copy(1, 1, b).wait_send()
 

time: 75.4 us -> 74.1 us (0.983)
  Pallas kernels: 73.2 us -> 72 us
    pallas_call x1, Pallas kernels: 70.7 us -> 69.4 us  [per_device(): pl.pallas_call(functools.partial(kernel, n_ctx, groups), out_shape=jax.Sh...]
where the time goes in v6:
time: 74.1 us; the launch traced here: 73.9 us
  Pallas kernels  72 us (97%)
  local copies, waits for them, and re-layouts  1.31 us (2%)
    pallas_call x1, Pallas kernels, per_device(): pl.pallas_call(functools.partial(kernel, n_ctx, groups), out_shape=jax.Sh...  69.4 us
    pallas_call x1, Pallas kernels, per_device(): pl.pallas_call(spread, out_shape=(tile,) * 4, in_specs=[vmem_spec], out_s...  2.58 us

profile of v6, /device:TPU:6, one launch (start us, length us, event | category | flops | bytes accessed | tf_op | source)
XLA Modules:
  0.0 73.9 jit_solution(5140999356318948776)
XLA Ops:
  0.6 1.3 %pad_bitcast_fusion.offs = s32[24,128]{1,0:T(8,128)} fusion(s32[2056]{0:T(1024)} %param.11), kind=kLoop, calls=%fused_computation | loop fusion | bytes 20512 | tf_op jit(solution)/shard_map/reshape | solution.py:537
  1.9 69.4 %shard_map.93.all_ref = bf16[4,384,512]{2,1,0:T(8,128)(2,1)} custom-call(bf16[384,512]{1,0:T(8,128)(2,1)} %q_hbm.1, bf16[384,512]{1,0:T(8,128)(2,1)} %k_hbm.1, bf16[384,512]{1,0:T(8,128)(2,1)} %v_hbm.1, bf16[512,2048]{1,0:T(8,128)(2,1)} %w_hbm.1, bf16[384,512]{1,0:T(8,128)(2,1)} %c_hbm.1, s32[24,128]{1,0:T(8,128)} %pad_bitcast_fusion.offs), custom_call_target="tpu_custom_call" | custom-call | tf_op jit(solution)/shard_map/pallas_call | solution.py:542
  71.3 2.6 %shard_map.94 = (bf16[384,512]{1,0:T(8,128)(2,1)}, bf16[384,512]{1,0:T(8,128)(2,1)}, bf16[384,512]{1,0:T(8,128)(2,1)}, bf16[384,512]{1,0:T(8,128)(2,1)}) custom-call(bf16[4,384,512]{2,1,0:T(8,128)(2,1)} %shard_map.93.all_ref), custom_call_target="tpu_custom_call" | custom-call | tf_op jit(solution)/shard_map/pallas_call | solution.py:579
